TPU v7x, 512 devices: a whole 4x4x16 slice. The times are simulated.
512 devices in a mesh: dp: 16 (over y_hi, x, core), mp: 32 (over z, y_lo).
Axes of the slice: x: 4, y: 4 (y_hi: 2, y_lo: 2; y = y_hi * 2 + y_lo), z: 16, core: 2. Of those that a mesh axis runs over, the one named last changes fastest.
Arguments:
- hidden: bfloat16 [32768, 5120], P('dp', 'mp'), may hold values from -6 to 6
- mod_table: bfloat16 [50, 2, 5120], P(None, None, 'mp'), may hold values from -3 to 3
- timestep: int32 [16], P('dp'), may hold values from 0 to 49
- head_weight: bfloat16 [5120, 64], P('mp'), may hold values from -0.078125 to 0.078125
- conv_in: bfloat16 [16, 27, 384], replicated, may hold values from -0.3125 to 0.3125
- conv_mid: bfloat16 [384, 27, 384], P('dp'), may hold values from -0.0625 to 0.0625
- patch_weight: bfloat16 [384, 1024], replicated, may hold values from -0.3125 to 0.3125
- text_emb: float32 [16, 1024], P('dp'), may hold values from -6 to 6
Outputs:
- reward: float32 [16], P('dp')
- head_grad: float32 [5120, 64], P('mp')
- hidden_grad: bfloat16 [32768, 5120], P('dp', 'mp')
Inputs may be any that keep to these rules, and one draw needn't show every extreme that they name: One timestep index a video.
All inputs are finite; a program needn't handle non-finite values.
Results may differ from a plain program's by a relative error of at most 0.029.
Values may be sent and summed in bfloat16 or wider, within the bound.
A program may use at most 64 MiB of HBM per device.

v0:
```python
import jax
import jax.numpy as jnp
from jax import lax
from jax.sharding import PartitionSpec as P

LW = 64
LT = 2


def with_halo(block, sides, width):
    for axis, dim in sides:
        count = lax.axis_size(axis)
        forward = [(i, i + 1) for i in range(count - 1)]
        backward = [(target, source) for source, target in forward]
        low = lax.ppermute(
            lax.slice_in_dim(block, block.shape[dim] - width, None, axis=dim), axis, forward
        )
        high = lax.ppermute(lax.slice_in_dim(block, 0, width, axis=dim), axis, backward)
        block = jnp.concatenate([low, block, high], axis=dim)
    return block


def silu_slope(value):
    gate = jax.nn.sigmoid(value)
    return gate * (1.0 + value * (1.0 - gate))


def scoring(pooled, video_text, patch_weight):
    embedded = jnp.dot(pooled, patch_weight.astype(jnp.float32), precision=lax.Precision.HIGHEST)
    embed_length = jnp.sqrt(jnp.sum(embedded * embedded, axis=1) + 1e-06)
    text_length = jnp.sqrt(jnp.sum(video_text * video_text) + 1e-06)
    cosine = jnp.dot(embedded, video_text, precision=lax.Precision.HIGHEST) / (
        embed_length * text_length
    )
    return 100.0 * jnp.mean(cosine)


def make_views(rimmed, rows, reverse_time):
    time_pad = (0, 2) if reverse_time else (2, 0)
    padded = jnp.pad(rimmed, (time_pad, (0, 0), (1, 1), (0, 0)))
    frames, cols = (rimmed.shape[0], rimmed.shape[2])
    views = []
    for tap_index in range(27):
        step_time, step_rows, step_cols = (tap_index // 9, tap_index // 3 % 3, tap_index % 3)
        views.append(
            padded[
                step_time : step_time + frames,
                step_rows : step_rows + rows,
                step_cols : step_cols + cols,
            ]
        )
    return views


def backward_views(field):
    rimmed = with_halo(field, (("mp", 1),), 1)
    return make_views(rimmed, field.shape[1], True)


def forward_views(field):
    rimmed = with_halo(field, (("mp", 1),), 1)
    return make_views(rimmed, field.shape[1], False)


def forward_full(views, weight):
    summed = jnp.zeros(views[0].shape[:3] + (weight.shape[2],), jnp.float32)
    for tap_index in range(27):
        summed = summed + jnp.einsum(
            "thwi,io->thwo",
            views[tap_index],
            weight[:, tap_index, :],
            preferred_element_type=jnp.float32,
        )
    return summed


def backward_full(views, weight):
    summed = jnp.zeros(views[0].shape[:3] + (weight.shape[0],), jnp.float32)
    for tap_index in range(27):
        summed = summed + jnp.einsum(
            "thwo,io->thwi",
            views[tap_index],
            weight[:, 26 - tap_index, :],
            preferred_element_type=jnp.float32,
        )
    return summed


def body(hidden, mod_table, timestep, head_weight, conv_in, conv_mid, patch_weight, text_emb):
    steps_total = mod_table.shape[0]
    selector = (jnp.arange(steps_total, dtype=jnp.int32) == timestep[0]).astype(jnp.float32)
    modulation = jnp.einsum(
        "s,skd->kd", selector, mod_table.astype(jnp.float32), precision=lax.Precision.HIGHEST
    )
    gain = 1.0 + modulation[1]
    modulated = (hidden.astype(jnp.float32) * gain + modulation[0]).astype(jnp.bfloat16)
    head_terms = jnp.dot(modulated, head_weight, preferred_element_type=jnp.float32)
    features = head_weight.shape[1]
    channels = features // 4
    video_tokens = hidden.shape[0]
    pair_cols = LW // 2
    pair_rows = video_tokens // (LT * pair_cols)
    latent_grid = head_terms.reshape(LT, pair_rows, pair_cols, features)
    narrow = lax.psum_scatter(
        latent_grid.astype(jnp.bfloat16), "mp", scatter_dimension=2, tiled=True
    )
    tile_rows = lax.all_to_all(narrow, "mp", split_axis=1, concat_axis=2, tiled=True)
    local_pairs = tile_rows.shape[1]
    local_rows = 2 * local_pairs
    latent = (
        tile_rows.reshape(LT, local_pairs, pair_cols, 2, 2, channels)
        .transpose(0, 1, 3, 2, 4, 5)
        .reshape(LT, local_rows, LW, channels)
    )
    pre_first = forward_full(forward_views(latent), conv_in)
    act_first = jax.nn.silu(pre_first).astype(jnp.bfloat16)
    mid_views = forward_views(act_first)
    gathered = lax.all_gather(conv_mid, "dp", axis=0, tiled=True)
    pre_second = forward_full(mid_views, gathered)
    decoded = jax.nn.silu(pre_second).astype(jnp.bfloat16)
    frame_sums = jnp.sum(decoded, axis=(1, 2), dtype=jnp.float32)
    cell_count = 2 * pair_rows * LW
    pooled = lax.psum(frame_sums, "mp") / cell_count
    video_text = text_emb[0]
    reward, pullback = jax.vjp(lambda pool_in: scoring(pool_in, video_text, patch_weight), pooled)
    pool_grad = pullback(jnp.ones((), jnp.float32))[0]
    grad_second = (pool_grad[:, None, None, :] / cell_count * silu_slope(pre_second)).astype(
        jnp.bfloat16
    )
    second_views = backward_views(grad_second)
    grad_act = backward_full(second_views, gathered)
    grad_first = (grad_act * silu_slope(pre_first)).astype(jnp.bfloat16)
    latent_grad = backward_full(backward_views(grad_first), conv_in).astype(jnp.bfloat16)
    full_grad = lax.all_gather(latent_grad, "mp", axis=1, tiled=True)
    token_grad = (
        full_grad.reshape(LT, pair_rows, 2, pair_cols, 2, channels)
        .transpose(0, 1, 3, 2, 4, 5)
        .reshape(video_tokens, features)
    )
    hidden_grad = (
        jnp.dot(token_grad, head_weight.T, preferred_element_type=jnp.float32) * gain
    ).astype(jnp.bfloat16)
    head_local = jnp.einsum("sd,sf->df", modulated, token_grad, preferred_element_type=jnp.float32)
    head_grad = lax.psum(head_local.astype(jnp.bfloat16), "dp").astype(jnp.float32)
    return (reward.reshape(1), head_grad, hidden_grad)


def solution(mesh):
    in_specs = (
        P("dp", "mp"),
        P(None, None, "mp"),
        P("dp"),
        P("mp", None),
        P(),
        P("dp", None, None),
        P(),
        P("dp", None),
    )
    out_specs = (P("dp"), P("mp", None), P("dp", "mp"))
    return jax.shard_map(body, mesh=mesh, in_specs=in_specs, out_specs=out_specs, check_vma=False)
```

profile of v0, /device:TPU:1, one launch (start us, length us, event | category | flops | bytes accessed | tf_op | source)
XLA Modules:
  0.0 487.1 jit_solution(5413933773133895783)
XLA Ops:
  9.8 1.5 convolution_convert_fusion
  18.9 132.0 %reduce-scatter.2.cloned.1.call-done = bf16[2,32,1,64]{3,1,0,2:T(8,128)(2,1)} async-done(((bf16[2,32,32,64]{3,1,0,2:T(8,128)(2,1)}), bf16[2,32,1,64]{3,1,0,2:T(8,128)(2,1)}) %reduce-scatter.2.cloned.1.call-update) | async-done | bytes 8208 | tf_op jit(solution)/shard_map/reduce_scatter | solution.py:104
  150.9 1.3 copy.25
  152.2 8.7 %all-to-all-start = ((bf16[2,32,1,64]{3,0,2,1:T(2,128)(2,1)}), bf16[2,32,1,64]{3,0,2,1:T(2,128)(2,1)S(1)}, u32[]{:S(2)}, u32[]{:S(2)}) async-start(bf16[2,32,1,64]{3,0,2,1:T(2,128)(2,1)} %copy.25), calls=%async_computation.1 | async-start | bytes 32768 | tf_op jit(solution)/shard_map/all_to_all | solution.py:107
  161.1 11.9 %all-to-all-done = bf16[2,32,1,64]{3,0,2,1:T(2,128)(2,1)S(1)} async-done(((bf16[2,32,1,64]{3,0,2,1:T(2,128)(2,1)}), bf16[2,32,1,64]{3,0,2,1:T(2,128)(2,1)S(1)}, u32[]{:S(2)}, u32[]{:S(2)}) %all-to-all-start) | async-done | bytes 8224 | tf_op jit(solution)/shard_map/all_to_all | solution.py:107
  173.4 2.3 collective-permute-start
  175.6 1.3 collective-permute-start.1
  177.1 2.9 collective-permute-done.1
  185.0 3.7 collective-permute-start.2
  188.8 1.3 collective-permute-start.3
  191.4 3.0 collective-permute-done.3
  194.6 1.4 fusion.65
  196.0 1.5 fusion.68
  211.3 46.9 %psum.14 = f32[2,384]{1,0:T(2,128)S(1)} all-reduce(f32[2,384]{1,0:T(2,128)S(1)} %get-tuple-element.18), channel_id=1, replica_groups=mesh['dp'=16,'mp'=32] {'mp'}, use_global_device_ids=true, to_apply=%region_2.3 | all-reduce | flops 768 | bytes 6144 | tf_op jit(solution)/shard_map/psum | solution.py:123
  260.5 2.5 collective-permute-start.4
  263.0 1.5 collective-permute-start.5
  264.6 3.8 collective-permute-done.5
  269.9 1.3 fusion.71
  271.1 1.3 fusion.72
  272.4 1.3 fusion.67
  274.9 1.4 fusion.21
  276.3 1.3 convolution_add_fusion.45
  277.6 1.3 convolution_add_fusion.44
  280.1 1.3 fusion.23
  286.5 2.7 collective-permute-start.6
  289.3 1.3 collective-permute-start.7
  291.2 3.4 collective-permute-done.7
  299.9 51.4 %all_gather.7 = bf16[2,64,64,16]{2,3,1,0:T(8,128)(2,1)S(1)} all-gather(bf16[2,2,64,16]{2,3,1,0:T(8,128)(2,1)S(1)} %fusion.31), channel_id=1, replica_groups=mesh['dp'=16,'mp'=32] {'mp'}, dimensions={1}, use_global_device_ids=true | all-gather | bytes 270336 | tf_op jit(solution)/shard_map/all_gather | solution.py:134
  352.3 3.7 copy.35
  356.1 2.4 reshape.33
  359.7 1.5 convolution_convert_fusion.1
  361.2 116.7 %psum.15 = bf16[160,64]{0,1:T(8,128)(2,1)S(1)} all-reduce(bf16[160,64]{0,1:T(8,128)(2,1)S(1)} %convolution_convert_fusion.1), channel_id=1, replica_groups=mesh['dp'=16,'mp'=32] {'dp'}, use_global_device_ids=true, to_apply=%region_6.7 | all-reduce | flops 10240 | bytes 40960 | tf_op jit(solution)/shard_map/psum | solution.py:144
  (147 shorter events, 47.8 us)
Async XLA Ops:
  8.0 250.3 %copy-start = (bf16[384,1024]{1,0:T(8,128)(2,1)S(1)}, bf16[384,1024]{1,0:T(8,128)(2,1)}, u32[]{:S(2)}) copy-start(bf16[384,1024]{1,0:T(8,128)(2,1)} %param.14) | copy-start | bytes 2359300
  8.0 10.5 %copy-start.2 = (bf16[16,27,384]{2,0,1:T(8,128)(2,1)S(1)}, bf16[16,27,384]{2,0,1:T(8,128)(2,1)}, u32[]{:S(2)}) copy-start(bf16[16,27,384]{2,0,1:T(8,128)(2,1)} %param.12) | copy-start | bytes 995332
  8.0 142.9 %reduce-scatter.2.cloned.1.call-start = ((), (), s32[]{:S(2)}) async-start(), calls=%async_computation.3 | async-start | bytes 540672 | tf_op jit(solution)/shard_map/reduce_scatter | solution.py:104
  12.6 182.1 %all-gather.2.cloned.1.call-start = ((), (), s32[]{:S(2)}) async-start(), calls=%async_computation.2 | async-start | bytes 8460288 | tf_op jit(solution)/shard_map/all_gather | solution.py:118
  152.2 20.9 %all-to-all-start = ((bf16[2,32,1,64]{3,0,2,1:T(2,128)(2,1)}), bf16[2,32,1,64]{3,0,2,1:T(2,128)(2,1)S(1)}, u32[]{:S(2)}, u32[]{:S(2)}) async-start(bf16[2,32,1,64]{3,0,2,1:T(2,128)(2,1)} %copy.25), calls=%async_computation.1 | async-start | bytes 32768 | tf_op jit(solution)/shard_map/all_to_all | solution.py:107
  173.4 16.7 %copy-start.4 = (f32[1,1024]{1,0:T(1,128)S(1)}, f32[1,1024]{1,0:T(1,128)}, u32[]{:S(2)}) copy-start(f32[1,1024]{1,0:T(1,128)} %param.15) | copy-start | bytes 12292
  173.4 3.7 collective-permute-start
  175.6 4.4 collective-permute-start.1
  185.0 6.3 %collective-permute-start.2 = (bf16[2,1,64,384]{3,2,1,0:T(8,128)(2,1)S(1)}, bf16[2,1,64,384]{3,2,1,0:T(8,128)(2,1)S(1)}, u32[]{:S(2)}, u32[]{:S(2)}) collective-permute-start(bf16[2,1,64,384]{3,2,1,0:T(8,128)(2,1)S(1)} %get-tuple-element.7), channel_id=1, source_target_pairs={{0,1},{1,2},{2,3},{3,4},{4,5},{5,6},{6,7},{7,8},{8,9},{9,10},{10,1... | collective-permute-start | bytes 294920 | tf_op jit(solution)/shard_map/ppermute | solution.py:15
  188.8 5.7 %collective-permute-start.3 = (bf16[2,1,64,384]{3,2,1,0:T(8,128)(2,1)S(1)}, bf16[2,1,64,384]{3,2,1,0:T(8,128)(2,1)S(1)}, u32[]{:S(2)}, u32[]{:S(2)}) collective-permute-start(bf16[2,1,64,384]{3,2,1,0:T(8,128)(2,1)S(1)} %get-tuple-element.8), channel_id=1, source_target_pairs={{1,0},{2,1},{3,2},{4,3},{5,4},{6,5},{7,6},{8,7},{9,8},{10,9},{11,1... | collective-permute-start | bytes 294920 | tf_op jit(solution)/shard_map/ppermute | solution.py:18
  194.6 11.6 %copy-start.1 = (bf16[384,27,384]{2,0,1:T(8,128)(2,1)S(1)}, bf16[384,27,384]{2,0,1:T(8,128)(2,1)}, u32[]{:S(2)}) copy-start(bf16[384,27,384]{2,0,1:T(8,128)(2,1)} %all-gather.2.cloned.1.call-done) | copy-start | bytes 23887876
  258.8 22.6 %slice-start = ((s8[7962624]{0:T(1024)(128)(4,1)}), s8[3768320]{0:T(1024)(128)(4,1)S(1)}, s32[]{:S(2)}) async-start(s8[7962624]{0:T(1024)(128)(4,1)} %bitcast.496), calls=%async_computation.4 | async-start | bytes 7536640
  260.5 4.1 collective-permute-start.4
  263.0 5.4 %collective-permute-start.5 = (bf16[2,1,64,384]{3,2,1,0:T(8,128)(2,1)S(1)}, bf16[2,1,64,384]{3,2,1,0:T(8,128)(2,1)S(1)}, u32[]{:S(2)}, u32[]{:S(2)}) collective-permute-start(bf16[2,1,64,384]{3,2,1,0:T(8,128)(2,1)S(1)} %get-tuple-element.6), channel_id=1, source_target_pairs={{1,0},{2,1},{3,2},{4,3},{5,4},{6,5},{7,6},{8,7},{9,8},{10,9},{11,1... | collective-permute-start | bytes 294920 | tf_op jit(solution)/shard_map/ppermute | solution.py:18
  274.9 6.5 %slice-start.1 = ((s8[7962624]{0:T(1024)(128)(4,1)}), s8[4194304]{0:T(1024)(128)(4,1)S(1)}, s32[]{:S(2)}) async-start(s8[7962624]{0:T(1024)(128)(4,1)} %bitcast.496), calls=%async_computation.5 | async-start | bytes 8388608
  286.5 4.7 collective-permute-start.6
  289.3 5.4 %collective-permute-start.7 = (bf16[2,1,64,384]{3,2,1,0:T(8,128)(2,1)S(1)}, bf16[2,1,64,384]{3,2,1,0:T(8,128)(2,1)S(1)}, u32[]{:S(2)}, u32[]{:S(2)}) collective-permute-start(bf16[2,1,64,384]{3,2,1,0:T(8,128)(2,1)S(1)} %get-tuple-element.4), channel_id=1, source_target_pairs={{1,0},{2,1},{3,2},{4,3},{5,4},{6,5},{7,6},{8,7},{9,8},{10,9},{11,1... | collective-permute-start | bytes 294920 | tf_op jit(solution)/shard_map/ppermute | solution.py:18
  291.2 67.3 %copy-start.3 = (bf16[160,64]{0,1:T(8,128)(2,1)S(1)}, bf16[160,64]{0,1:T(8,128)(2,1)}, u32[]{:S(2)}) copy-start(bf16[160,64]{0,1:T(8,128)(2,1)} %param.11) | copy-start | bytes 61444
Sparse Core Ops, SparseCore 0:
  12.7 138.1 reduce-scatter.1
Sparse Core Ops, SparseCore 1:
  16.4 92.6 all-gather.1
where the time goes:
time: 494 us; the launch traced here: 487 us
  blocking collectives  215 us (44%)
  waiting for transfers between devices  158 us (32%)
  matrix products  57.2 us (12%)
  starting transfers between devices  25.3 us (5%)
  between operations  19.6 us (4%)
  local copies, waits for them, and re-layouts  10.1 us (2%)
    reduce_scatter x1, waiting for transfers between devices, body(): lax.psum_scatter(latent_grid.astype(jnp.bfloat16), 'mp', scatter_dimensio...  132 us
    psum x1, blocking collectives, body(): lax.psum(head_local.astype(jnp.bfloat16), 'dp').astype(jnp.float32)  117 us
    all_gather x1, blocking collectives, body(): full_grad = lax.all_gather(latent_grad, 'mp', axis=1, tiled=True)  51.4 us
    psum x1, blocking collectives, body(): pooled = lax.psum(frame_sums, 'mp') / cell_count  46.9 us
    dot_general x54, matrix products, forward_full(): jnp.einsum('thwi,io->thwo', views[tap_index], weight[:, tap_index, :], pr...  27.2 us
    dot_general x54, matrix products, backward_full(): jnp.einsum('thwo,io->thwi', views[tap_index], weight[:, 26 - tap_index, :...  22.8 us
    ppermute x4, waiting for transfers between devices, with_halo(): lax.ppermute(lax.slice_in_dim(block, 0, width, axis=dim), axis, backward)  13.2 us
    all_to_all x1, waiting for transfers between devices, body(): lax.all_to_all(narrow, 'mp', split_axis=1, concat_axis=2, tiled=True)  11.9 us
  transfers between devices with their start and end apart: 11, of which 7 were waited for; matrix products, arithmetic and copies ran while one was open for 3% of the time, Pallas kernels for 0%

commit v1 on v0

v1 whole, which is shorter than its diff:
```python
import jax
import jax.numpy as jnp
from jax import lax
from jax.experimental import pallas as pl
from jax.experimental.pallas import tpu as pltpu
from jax.sharding import PartitionSpec as P

F32 = jnp.float32
BF16 = jnp.bfloat16
NMP = 32
NDP = 16
FEAT = 160
Q = 32
C = 16
CH = 384
EMB = 1024
CELLS = 4096
SHARD = 48
OWNERS = 8
NT = (((1,), (1,)), ((), ()))


def window_placement():
    source = lax.broadcasted_iota(jnp.int32, (384, 1), 0)
    frame, row, col = (lax.rem(source, 2 * n) // n for n in (64, 32, 16))
    px = 2 * (source // 128) + col - 1
    there = (px >= 0) & (px < 4)
    at = row * 128 + px * 16 + lax.rem(source, 16)
    full = jnp.where(there, at + frame * 64, -1)
    shifted = jnp.where(there & (frame == 0), at + 256 + 64, -1)
    lane = lax.broadcasted_iota(jnp.int32, (384, 512), 1)
    return jnp.where((lane == full) | (lane == shifted), 1.0, 0.0).astype(BF16)


def dot(a, b, dims=(((1,), (0,)), ((), ()))):
    return lax.dot_general(a, b, dims, preferred_element_type=F32)


def sigmoid(value):
    return 1.0 / (1.0 + jnp.exp(-value))


def three_parts(value):
    high = value.astype(BF16)
    rest = value - high.astype(F32)
    middle = rest.astype(BF16)
    low = (rest - middle.astype(F32)).astype(BF16)
    rows = [high.astype(F32), middle.astype(F32), low.astype(F32), jnp.zeros_like(value)]
    return jnp.concatenate(rows, axis=0).astype(BF16)


def from_previous(value):
    rows = value.shape[0]
    inside = lax.rem(lax.broadcasted_iota(jnp.int32, (rows, 1), 0), Q) != 0
    return jnp.where(inside, pltpu.roll(value, 1, 0), 0.0)


def from_next(value):
    rows = value.shape[0]
    inside = lax.rem(lax.broadcasted_iota(jnp.int32, (rows, 1), 0), Q) != Q - 1
    return jnp.where(inside, pltpu.roll(value, rows - 1, 0), 0.0)


def rows_inside(rows, first_row):
    row = lax.broadcasted_iota(jnp.int32, (rows, 1), 0) // Q + first_row
    return jnp.where((row >= 0) & (row < 2 * NMP), 1.0, 0.0).astype(F32)


def spread(ref, frame, even, odd, reverse):
    rows = even.shape[0] // Q
    before_even = from_previous(odd).astype(BF16).reshape(rows, Q, CH)
    after_odd = from_next(even).astype(BF16).reshape(rows, Q, CH)
    even = even.astype(BF16).reshape(rows, Q, CH)
    odd = odd.astype(BF16).reshape(rows, Q, CH)
    low, high = (2, 0) if reverse else (0, 2)
    ref[frame, :, 0:Q, low * CH : (low + 1) * CH] = before_even
    ref[frame, :, 0:Q, CH : 2 * CH] = even
    ref[frame, :, 0:Q, high * CH : (high + 1) * CH] = odd
    ref[frame, :, Q : 2 * Q, low * CH : (low + 1) * CH] = even
    ref[frame, :, Q : 2 * Q, CH : 2 * CH] = odd
    ref[frame, :, Q : 2 * Q, high * CH : (high + 1) * CH] = after_odd


def kernel(
    step_ref,
    hidden_ref,
    mod_ref,
    head_ref,
    cin_ref,
    cmid_ref,
    patch_ref,
    text_ref,
    reward_ref,
    head_grad_ref,
    hidden_grad_ref,
    modulated,
    head_wide,
    place,
    parts_out,
    parts_in,
    latents,
    windows,
    first_weight,
    first_back,
    field,
    second,
    slope_first,
    back_field,
    back_first,
    weights,
    sibling_out,
    sibling_in,
    pooled_all,
    grads,
    hidden_out,
    head_out,
    head_in,
    head_sum,
    sib_sems,
    parts_sems,
    halo_send,
    halo_recv,
    w_send,
    w_recv,
    s_recv,
    pool_sems,
    grad_sems,
    head_sems,
    total_sems,
    out_sem,
):
    dp = lax.axis_index("dp")
    mp = lax.axis_index("mp")
    core = lax.rem(dp, 2)
    x = lax.rem(dp // 2, 4)
    y_hi = dp // 8
    y_lo = lax.rem(mp, 2)
    right_x, left_x, far_x = lax.rem(x + 1, 4), lax.rem(x + 3, 4), lax.rem(x + 2, 4)
    sibling = dp + 1 - 2 * core
    right = y_hi * 8 + right_x * 2 + core
    left = y_hi * 8 + left_x * 2 + core
    other_dp = (1 - y_hi) * 8 + x * 2 + core
    other_mp = mp + 1 - 2 * y_lo
    mine, beside = y_hi * 4, (1 - y_hi) * 4

    def send(src, dst, send_sem, recv_sem, to_dp, to_mp):
        pltpu.make_async_remote_copy(
            src_ref=src,
            dst_ref=dst,
            send_sem=send_sem,
            recv_sem=recv_sem,
            device_id=(to_dp, to_mp),
            device_id_type=pl.DeviceIdType.MESH,
        ).start()

    def wait(ref, sem):
        pltpu.make_async_copy(ref, ref, sem).wait()

    barrier = pltpu.get_barrier_semaphore()

    def greet(to_dp, to_mp):
        pl.semaphore_signal(
            barrier, inc=1, device_id=(to_dp, to_mp), device_id_type=pl.DeviceIdType.MESH
        )

    @pl.loop(1, NMP)
    def _(d):
        greet(dp, lax.rem(mp + d, NMP))

    @pl.loop(1, NDP)
    def _(d):
        greet(lax.rem(dp + d, NDP), mp)

    greet(other_dp, other_mp)

    modulation = mod_ref[step_ref[0]].astype(F32)
    across = lax.broadcasted_iota(jnp.int32, (FEAT, FEAT), 1)
    diagonal = lax.broadcasted_iota(jnp.int32, (FEAT, FEAT), 0) == across
    shift, gain = (
        jnp.sum(jnp.where(diagonal, modulation[n : n + 1], 0.0), axis=1, keepdims=True)
        for n in range(2)
    )
    gain = 1.0 + gain

    @pl.loop(0, 4)
    def _(n):
        halves = []
        for f in range(2):
            columns = pl.ds(pl.multiple_of(n * 256 + f * 1024, 256), 256)
            block = (hidden_ref[:, columns].astype(F32) * gain + shift).astype(BF16)
            modulated[:, columns] = block
            halves.append(dot(head_ref[...], block))
        total = jnp.concatenate(halves, axis=0).T
        parts_out[pl.ds(n * 8, 8)] = total.astype(BF16).reshape(8, Q, 128)

    @pl.loop(0, 18)
    def _(t):
        own = cmid_ref[t + 9].astype(F32)
        sibling_out[t] = jnp.concatenate([own, jnp.zeros((8, CH), F32)], axis=0).astype(BF16)

    pl.semaphore_wait(barrier, NMP - 1 + NDP - 1 + 1)

    send(sibling_out, sibling_in, sib_sems.at[0], sib_sems.at[1], sibling, mp)

    @pl.loop(1, NMP)
    def _(d):
        to = lax.rem(mp + d, NMP)
        send(parts_out.at[to], parts_in.at[NMP - 1 - d], parts_sems.at[0], parts_sems.at[1], dp, to)

    wait(sibling_in, sib_sems.at[1])

    def shard_rows(j):
        return pl.ds(pl.multiple_of(SHARD * j, 16), SHARD)

    own_rows = shard_rows(dp // 2)

    @pl.loop(0, 18)
    def _(t):
        own = sibling_out[t].astype(F32)
        other = sibling_in[t].astype(F32)
        low = jnp.where(core == 0, own, other)
        high = jnp.where(core == 0, other, own)
        weights[t, own_rows, :] = jnp.concatenate([low[0:24], high[0:24]], axis=0).astype(BF16)

    def piece(i, j, c):
        return weights.at[pl.ds(3 * (2 * i + c), 3), shard_rows(j), :]

    def pass_on(i, j, kind, to_dp, to_mp):
        block = piece(i, j, core)
        send(block, block, w_send, w_recv.at[kind, i], to_dp, to_mp)

    def hand_over(i, j, kind):
        block = piece(i, j, core)
        send(block, block, w_send, s_recv.at[kind, i], sibling, mp)

    def arrived(i, j, kind):
        wait(piece(i, j, core), w_recv.at[kind, i])
        hand_over(i, j, kind)

    BESIDE, LEFT, RIGHT, LEFT2, RIGHT2, FAR, FAR2 = range(7)
    own = mine + x
    kinds = (
        (BESIDE, beside + x),
        (LEFT, mine + left_x),
        (RIGHT, mine + right_x),
        (LEFT2, beside + left_x),
        (RIGHT2, beside + right_x),
        (FAR, mine + far_x),
        (FAR2, beside + far_x),
    )
    for i in range(3):
        pass_on(i, own, BESIDE, other_dp, other_mp)
        pass_on(i, own, LEFT, right, mp)
        pass_on(i, own, RIGHT, left, mp)

    first_weight[...] = jnp.zeros_like(first_weight)
    for a in range(2):
        for b in range(3):
            for c in range(3):
                tap = cin_ref[9 + 9 * a + 3 * b + c]
                for j in range(2):
                    at = b * 128 + a * 64 + (c + j) * 16
                    first_weight[at : at + 16, j * CH : (j + 1) * CH] = tap
                at = (a * 3 + b) * 16
                first_back[at : at + 16, c * CH : (c + 1) * CH] = tap

    for f in range(2):
        head_wide[f] = jnp.zeros((FEAT, 128), BF16)
        head_wide[f, :, f * 64 : (f + 1) * 64] = head_ref[...].astype(F32).T.astype(BF16)
    place[...] = window_placement()

    for i in range(3):
        arrived(i, beside + x, BESIDE)
        pass_on(i, beside + x, LEFT2, right, mp)
        pass_on(i, beside + x, RIGHT2, left, mp)
    for i in range(3):
        arrived(i, mine + left_x, LEFT)
        pass_on(i, mine + left_x, FAR, right, mp)
        arrived(i, mine + right_x, RIGHT)

    wait(parts_in, parts_sems.at[1])
    latent = parts_out[mp].astype(F32)
    for s in range(NMP - 1):
        latent = latent + parts_in[s].astype(F32)
    latents[2] = latent.astype(BF16)
    for n, d in enumerate((-2, -1, 1, 2)):
        to = lax.rem(mp + d + NMP, NMP)
        send(latents.at[2], latents.at[2 - d], halo_send.at[n], halo_recv.at[n], dp, to)
    for n, d in enumerate((-2, -1, 1, 2)):
        wait(latents.at[2 - d], halo_recv.at[n])

    pair = lax.broadcasted_iota(jnp.int32, (5 * Q, 1), 0) // Q + mp - 2
    tokens = jnp.where((pair >= 0) & (pair < NMP), latents[...].reshape(5 * Q, 128).astype(F32), 0.0)
    around = jnp.concatenate([from_previous(tokens), tokens, from_next(tokens)], axis=1)
    placed = dot(around.astype(BF16), place[...]).astype(BF16)
    for p in range(5):
        for row in range(2):
            rows = slice(p * Q, (p + 1) * Q)
            windows[1, 2 * p + row] = placed[rows, row * 128 : (row + 1) * 128]
            windows[0, 2 * p + row] = placed[rows, 256 + row * 128 : 256 + (row + 1) * 128]
    for f in range(2):
        taps = jnp.concatenate([windows[f, b : b + 8].reshape(8 * Q, 128) for b in range(3)], axis=1)
        inside = rows_inside(8 * Q, 2 * mp - 3)
        columns = []
        for j in range(2):
            value = dot(taps, first_weight[:, j * CH : (j + 1) * CH])
            gate = sigmoid(value)
            columns.append(value * gate * inside)
            slope = gate * (1.0 + value * (1.0 - gate))
            slope_first[f, :, j * Q : (j + 1) * Q, :] = slope[2 * Q : 6 * Q].reshape(4, Q, CH)
        spread(field, f, columns[0], columns[1], False)

    for i in range(3):
        arrived(i, beside + left_x, LEFT2)
        arrived(i, beside + right_x, RIGHT2)
        pass_on(i, beside + right_x, FAR2, left, mp)
    for i in range(3):
        arrived(i, mine + far_x, FAR)
        arrived(i, beside + far_x, FAR2)

    for i in range(3):
        for kind, j in kinds:
            wait(piece(i, j, 1 - core), s_recv.at[kind, i])
        for g in (2 * i, 2 * i + 1):
            a, b = g // 3, g % 3
            weight = weights[3 * g : 3 * g + 3].reshape(3 * CH, CH)
            for f in range(1 - a, 2):
                source = field[f + a - 1, b : b + 6].reshape(6 * 64, 3 * CH)
                value = dot(source, weight)
                if (g, f) in ((0, 1), (3, 0)):
                    second[f] = value
                else:
                    second[f] = second[f] + value

    pooled_all[mp] = jnp.zeros((8, 128), F32)
    for f in range(2):
        value = second[f, 128:256]
        decoded = (value * sigmoid(value)).astype(BF16).astype(F32)
        sums = jnp.sum(decoded, axis=0, keepdims=True)
        for n in range(3):
            pooled_all[mp, 3 * f + n : 3 * f + n + 1, :] = sums[:, n * 128 : (n + 1) * 128]

    @pl.loop(1, NMP)
    def _(d):
        to = lax.rem(mp + d, NMP)
        send(pooled_all.at[mp], pooled_all.at[mp], pool_sems.at[0], pool_sems.at[1], dp, to)

    row = lax.broadcasted_iota(jnp.int32, (6 * 64, 1), 0) // 64 + 2 * mp - 2
    inside = jnp.where((row >= 0) & (row < 2 * NMP), 1.0, 0.0)
    for f in range(2):
        value = second[f]
        gate = sigmoid(value)
        second[f] = gate * (1.0 + value * (1.0 - gate)) * inside

    wait(pooled_all.at[pl.ds(0, NMP - 1)], pool_sems.at[1])

    sums = pooled_all[0]
    for s in range(1, NMP):
        sums = sums + pooled_all[s]
    sums = sums * (1.0 / CELLS)
    frames = [jnp.concatenate([sums[3 * f + n : 3 * f + n + 1] for n in range(3)], axis=1) for f in range(2)]
    pooled = jnp.concatenate(frames, axis=0)
    rows = dot(three_parts(pooled), patch_ref[...])
    embedded = rows[0:2] + rows[2:4] + rows[4:6]
    text = text_ref[...]
    embed_square = jnp.sum(embedded * embedded, axis=1, keepdims=True) + 1e-6
    embed_scale = lax.rsqrt(embed_square)
    text_scale = lax.rsqrt(jnp.sum(text * text, axis=1, keepdims=True) + 1e-6)
    cosine = jnp.sum(embedded * text, axis=1, keepdims=True) * embed_scale * text_scale
    reward_ref[...] = jnp.broadcast_to(50.0 * (cosine[0:1] + cosine[1:2]), (1, 128))
    embed_grad = 50.0 * embed_scale * (text * text_scale - embedded * (cosine * embed_scale))
    rows = dot(three_parts(embed_grad), patch_ref[...], NT)
    pool_grad = (rows[0:2] + rows[2:4] + rows[4:6]) * (1.0 / CELLS)

    for f in range(2):
        grad = (second[f] * pool_grad[f : f + 1]).reshape(6, 64, CH)
        spread(back_field, f, grad[:, 0:Q].reshape(6 * Q, CH), grad[:, Q:].reshape(6 * Q, CH), True)
    row = lax.broadcasted_iota(jnp.int32, (4 * 64, 1), 0) // 64 + 2 * mp - 1
    inside = jnp.where((row >= 0) & (row < 2 * NMP), 1.0, 0.0)
    for f in range(2):
        total = None
        for a in range(f, 2):
            for b in range(3):
                source = back_field[f + 1 - a, 2 - b : 6 - b].reshape(4 * 64, 3 * CH)
                for c in range(3):
                    term = dot(source[:, c * CH : (c + 1) * CH], weights[9 * a + 3 * b + c], NT)
                    total = term if total is None else total + term
        total = total * slope_first[f].reshape(4 * 64, CH) * inside
        total = total.reshape(4, 64, CH)
        spread(back_first, f, total[:, 0:Q].reshape(4 * Q, CH), total[:, Q:].reshape(4 * Q, CH), True)

    taps = [dot(back_first[f].reshape(4 * 64, 3 * CH), first_back[...], NT) for f in range(2)]
    blocks = []
    for f in range(2):
        for i in range(2):
            for j in range(2):
                total = None
                for a in range(2):
                    if f + 1 - a > 1:
                        continue
                    for b in range(3):
                        at = (i + 2 - b) * 64 + j * Q
                        lane = (a * 3 + b) * 16
                        term = taps[f + 1 - a][at : at + Q, lane : lane + 16]
                        total = term if total is None else total + term
                blocks.append(total)
    grads[mp] = jnp.concatenate(blocks, axis=1).astype(BF16)

    @pl.loop(1, NMP)
    def _(d):
        to = lax.rem(mp + d, NMP)
        send(grads.at[mp], grads.at[mp], grad_sems.at[0], grad_sems.at[1], dp, to)

    wait(grads.at[pl.ds(0, NMP - 1)], grad_sems.at[1])
    token_grad = grads[...].reshape(NMP * Q, 128)

    early = dot(modulated[:, 0:1024], token_grad).T
    late = dot(modulated[:, 1024:2048], token_grad).T
    head_out[...] = early[0:64] + late[64:128]

    @pl.loop(0, OWNERS)
    def _(c):
        @pl.when(c != dp)
        def _():
            block = head_out.at[pl.ds(pl.multiple_of(8 * c, 8), 8)]
            send(block, head_in.at[dp], head_sems.at[0], head_sems.at[1], c, mp)

    def hidden_part(f):
        value = dot(head_wide[f], grads[...].reshape(NMP * Q, 128), NT) * gain
        hidden_out[:, f * 1024 : (f + 1) * 1024] = value.astype(BF16)
        columns = pl.ds(f * 1024, 1024)
        pltpu.make_async_copy(
            hidden_out.at[:, columns], hidden_grad_ref.at[:, columns], out_sem.at[f]
        ).start()

    hidden_part(0)
    own_block = pl.ds(pl.multiple_of(8 * jnp.minimum(dp, OWNERS - 1), 8), 8)

    @pl.when(dp < OWNERS)
    def _():
        head_in[dp] = head_out[own_block, :]
        wait(head_in.at[pl.ds(0, NDP - 1)], head_sems.at[1])
        total = head_in[0]
        for s in range(1, NDP):
            total = total + head_in[s]
        head_sum[own_block, :] = total

        @pl.loop(1, NDP)
        def _(d):
            block = head_sum.at[own_block]
            send(block, block, total_sems.at[0], total_sems.at[1], lax.rem(dp + d, NDP), mp)

    hidden_part(1)

    @pl.when(dp < OWNERS)
    def _():
        wait(head_sum.at[pl.ds(0, 8 * (OWNERS - 1))], total_sems.at[1])
        wait(head_in.at[pl.ds(0, NDP - 1)], total_sems.at[0])
        wait(head_out.at[pl.ds(0, 8 * (OWNERS - 1))], head_sems.at[0])

    @pl.when(dp >= OWNERS)
    def _():
        wait(head_sum, total_sems.at[1])
        wait(head_out, head_sems.at[0])

    head_grad_ref[...] = head_sum[...]

    wait(sibling_out, sib_sems.at[0])
    wait(parts_in, parts_sems.at[0])
    for n in range(4):
        wait(latents.at[2], halo_send.at[n])
    wait(weights.at[:, pl.ds(0, 7 * SHARD), :], w_send)
    wait(pooled_all.at[pl.ds(0, NMP - 1)], pool_sems.at[0])
    wait(grads.at[pl.ds(0, NMP - 1)], grad_sems.at[0])
    for f in range(2):
        columns = pl.ds(f * 1024, 1024)
        pltpu.make_async_copy(
            hidden_out.at[:, columns], hidden_grad_ref.at[:, columns], out_sem.at[f]
        ).wait()


def body(hidden, mod_table, timestep, head_weight, conv_in, conv_mid, patch_weight, text_emb):
    vmem = pl.BlockSpec(memory_space=pltpu.VMEM)
    dma = pltpu.SemaphoreType.DMA
    reward, head_grad, hidden_grad = pl.pallas_call(
        kernel,
        out_shape=(
            jax.ShapeDtypeStruct((1, 128), F32),
            jax.ShapeDtypeStruct((64, FEAT), F32),
            jax.ShapeDtypeStruct((FEAT, 2048), BF16),
        ),
        in_specs=[pl.BlockSpec(memory_space=pltpu.SMEM)] + [vmem] * 7,
        out_specs=(vmem, vmem, pl.BlockSpec(memory_space=pl.ANY)),
        scratch_shapes=[
            pltpu.VMEM((FEAT, 2048), BF16),
            pltpu.VMEM((2, FEAT, 128), BF16),
            pltpu.VMEM((384, 512), BF16),
            pltpu.VMEM((NMP, Q, 128), BF16),
            pltpu.VMEM((NMP - 1, Q, 128), BF16),
            pltpu.VMEM((5, Q, 128), BF16),
            pltpu.VMEM((2, 10, Q, 128), BF16),
            pltpu.VMEM((384, 2 * CH), BF16),
            pltpu.VMEM((96, 3 * CH), BF16),
            pltpu.VMEM((2, 8, 64, 3 * CH), BF16),
            pltpu.VMEM((2, 6 * 64, CH), F32),
            pltpu.VMEM((2, 4, 64, CH), F32),
            pltpu.VMEM((2, 6, 64, 3 * CH), BF16),
            pltpu.VMEM((2, 4, 64, 3 * CH), BF16),
            pltpu.VMEM((18, CH, CH), BF16),
            pltpu.VMEM((18, 32, CH), BF16),
            pltpu.VMEM((18, 32, CH), BF16),
            pltpu.VMEM((NMP, 8, 128), F32),
            pltpu.VMEM((NMP, Q, 128), BF16),
            pltpu.VMEM((FEAT, 2048), BF16),
            pltpu.VMEM((64, FEAT), F32),
            pltpu.VMEM((NDP, 8, FEAT), F32),
            pltpu.VMEM((64, FEAT), F32),
            dma((2,)),
            dma((2,)),
            dma((4,)),
            dma((4,)),
            dma,
            dma((7, 3)),
            dma((7, 3)),
            dma((2,)),
            dma((2,)),
            dma((2,)),
            dma((2,)),
            dma((2,)),
        ],
        compiler_params=pltpu.CompilerParams(
            collective_id=0, has_side_effects=True, vmem_limit_bytes=48 * 1024 * 1024
        ),
        name="guided_step",
    )(
        timestep,
        hidden.T,
        mod_table,
        head_weight.T,
        jnp.transpose(conv_in, (1, 0, 2)),
        jnp.transpose(conv_mid, (1, 0, 2)),
        patch_weight,
        text_emb,
    )
    return (reward[0, 0:1], head_grad.T, hidden_grad.T)


def solution(mesh):
    in_specs = (
        P("dp", "mp"),
        P(None, None, "mp"),
        P("dp"),
        P("mp", None),
        P(),
        P("dp", None, None),
        P(),
        P("dp", None),
    )
    out_specs = (P("dp"), P("mp", None), P("dp", "mp"))
    return jax.shard_map(body, mesh=mesh, in_specs=in_specs, out_specs=out_specs, check_vma=False)
```

time: 494 us -> 104 us (0.21); the launches traced: 487 us -> 104 us
  blocking collectives: 215 us -> 0 us
  waiting for transfers between devices: 158 us -> 0 us
  Pallas kernels: 0 us -> 93.2 us
  matrix products: 57.2 us -> 0 us
  starting transfers between devices: 25.3 us -> 0 us
  between operations: 19.6 us -> 2.46 us
    psum x2 -> x0, blocking collectives: 164 us -> none  [the longest x1 117 us: body(): lax.psum(head_local.astype(jnp.bfloat16), 'dp').astype(jnp.float32)]
    reduce_scatter x1 -> x0, waiting for transfers between devices: 132 us -> none  [body(): lax.psum_scatter(latent_grid.astype(jnp.bfloat16), 'mp', scatter_dimensio...]
    pallas_call x0 -> x1, Pallas kernels: none -> 93.2 us  [body(): pl.pallas_call(kernel, out_shape=(jax.ShapeDtypeStruct((1, 128), F32), ja...]
    dot_general x115 -> x0, matrix products: 57.2 us -> none  [the longest x54 27.2 us: forward_full(): jnp.einsum('thwi,io->thwo', views[tap_index], weight[:, tap_index, :], pr...]
    all_gather x1 -> x0, blocking collectives: 51.4 us -> none  [body(): full_grad = lax.all_gather(latent_grad, 'mp', axis=1, tiled=True)]
    ppermute x8 -> x0, starting transfers between devices: 16.5 us -> none  [the longest x4 11.2 us: with_halo(): lax.ppermute(lax.slice_in_dim(block, block.shape[dim] - width, None, axis...]
    ppermute x8 -> x0, waiting for transfers between devices: 13.3 us -> none  [the longest x4 13.2 us: with_halo(): lax.ppermute(lax.slice_in_dim(block, 0, width, axis=dim), axis, backward)]
    all_to_all x1 -> x0, waiting for transfers between devices: 11.9 us -> none  [body(): lax.all_to_all(narrow, 'mp', split_axis=1, concat_axis=2, tiled=True)]
  transfers between devices with their start and end apart: 11 -> 0, of which waited for: 7 -> 0; matrix products, arithmetic and copies ran while one was open for 3% -> 0% of each run, Pallas kernels for 0% -> 0%
where the time goes in v1:
time: 104 us
  Pallas kernels  93.2 us (90%)
  local copies, waits for them, and re-layouts  7.93 us (8%)
  between operations  2.46 us (2%)
    pallas_call x1, Pallas kernels, body(): pl.pallas_call(kernel, out_shape=(jax.ShapeDtypeStruct((1, 128), F32), ja...  93.2 us
    unnamed x16, local copies, waits for them, and re-layouts  7.93 us

profile of v1, /device:TPU:1, one launch (start us, length us, event | category | flops | bytes accessed | tf_op | source)
XLA Modules:
  0.0 103.6 jit_solution(11119342576911355619)
XLA Ops:
  1.3 0.0 copy-start.6
  1.3 0.7 copy-done.6
  2.0 0.0 copy-start
  2.0 1.1 %copy-done = bf16[384,1024]{1,0:T(8,128)(2,1)S(1)} copy-done((bf16[384,1024]{1,0:T(8,128)(2,1)S(1)}, bf16[384,1024]{1,0:T(8,128)(2,1)}, u32[]{:S(2)}) %copy-start) | copy-done | bytes 786456
  3.1 0.0 copy-start.1
  3.1 1.1 %copy-done.1 = bf16[2048,160]{0,1:T(8,128)(2,1)S(1)} copy-done((bf16[2048,160]{0,1:T(8,128)(2,1)S(1)}, bf16[2048,160]{0,1:T(8,128)(2,1)}, u32[]{:S(2)}) %copy-start.1) | copy-done | bytes 655384
  4.2 0.0 copy-start.2
  4.2 1.0 copy-done.2
  5.2 0.0 copy-start.3
  5.2 1.0 copy-done.3
  6.2 0.0 copy-start.4
  6.2 0.8 copy-done.4
  7.0 0.0 copy-start.5
  7.0 0.8 copy-done.5
  7.8 93.2 %guided_step.1 = (f32[1,128]{1,0:T(1,128)S(1)}, f32[64,160]{1,0:T(8,128)S(1)}, bf16[160,2048]{1,0:T(8,128)(2,1)S(1)}) custom-call(s32[1]{0:T(128)S(6)} %copy.14.step_ref, bf16[160,2048]{1,0:T(8,128)(2,1)S(1)} %bitcast.8, bf16[50,2,160]{2,1,0:T(2,128)(2,1)S(1)} %copy-done.4, bf16[64,160]{1,0:T(8,128)(2,1)S(1)} %bitcast.13, bf16[27,16,384]{2,1,0:T(8,128)(2,1)S(1)} %bitcast.11, ...), custom_call_target="tpu_custom_call" | custom-call | tf_op jit(solution)/shard_map/guided_step/pallas_call | solution.py:485
  101.0 0.6 copy.16
  101.6 0.8 copy.17
Async XLA Ops:
  1.3 0.7 copy-start.6
  2.0 1.1 %copy-start = (bf16[384,1024]{1,0:T(8,128)(2,1)S(1)}, bf16[384,1024]{1,0:T(8,128)(2,1)}, u32[]{:S(2)}) copy-start(bf16[384,1024]{1,0:T(8,128)(2,1)} %patch_ref.1) | copy-start | bytes 2359300
  3.1 1.1 %copy-start.1 = (bf16[2048,160]{0,1:T(8,128)(2,1)S(1)}, bf16[2048,160]{0,1:T(8,128)(2,1)}, u32[]{:S(2)}) copy-start(bf16[2048,160]{0,1:T(8,128)(2,1)} %param.8) | copy-start | bytes 1966084
  4.2 1.0 copy-start.2
  5.2 1.0 copy-start.3
  6.2 0.8 copy-start.4
  7.0 0.8 copy-start.5

commit v2 on v1

--- a/solution.py
+++ b/solution.py
@@ -16,7 +16,7 @@
 EMB = 1024
 CELLS = 4096
 SHARD = 48
-OWNERS = 8
+NEAR = tuple((dz, dy) for dz in (2, 1, -1, 0) for dy in (0, 1) if (dz, dy) != (0, 0))
 NT = (((1,), (1,)), ((), ()))
 
 
@@ -83,21 +83,31 @@
 
 def kernel(
     step_ref,
+    hidden_far,
+    mod_far,
+    head_far,
+    cmid_far,
+    cin_far,
+    patch_far,
+    text_far,
+    reward_ref,
+    head_grad_ref,
+    hidden_grad_ref,
     hidden_ref,
     mod_ref,
     head_ref,
+    cmid_ref,
     cin_ref,
-    cmid_ref,
     patch_ref,
     text_ref,
-    reward_ref,
-    head_grad_ref,
-    hidden_grad_ref,
     modulated,
     head_wide,
     place,
     parts_out,
     parts_in,
+    sums_out,
+    sums_in,
+    own_sum,
     latents,
     windows,
     first_weight,
@@ -112,22 +122,22 @@
     sibling_in,
     pooled_all,
     grads,
-    hidden_out,
-    head_out,
     head_in,
-    head_sum,
     sib_sems,
-    parts_sems,
+    parts_send,
+    parts_recv,
+    sums_sems,
     halo_send,
     halo_recv,
     w_send,
     w_recv,
     s_recv,
     pool_sems,
-    grad_sems,
+    far_send,
+    far_recv,
+    near_sems,
     head_sems,
-    total_sems,
-    out_sem,
+    in_sems,
 ):
     dp = lax.axis_index("dp")
     mp = lax.axis_index("mp")
@@ -142,6 +152,14 @@
     other_dp = (1 - y_hi) * 8 + x * 2 + core
     other_mp = mp + 1 - 2 * y_lo
     mine, beside = y_hi * 4, (1 - y_hi) * 4
+    z = mp // 2
+    block_row, block_column = mp // 8, lax.rem(mp, 8)
+
+    def near(dz, dy):
+        return lax.rem(z + dz + 16, 16) * 2 + y_lo + dy * (1 - 2 * y_lo)
+
+    def far(dk):
+        return lax.rem(mp + 8 * dk, NMP)
 
     def send(src, dst, send_sem, recv_sem, to_dp, to_mp):
         pltpu.make_async_remote_copy(
@@ -156,6 +174,23 @@
     def wait(ref, sem):
         pltpu.make_async_copy(ref, ref, sem).wait()
 
+    loads = [
+        pltpu.make_async_copy(far, near, in_sems.at[n])
+        for n, (far, near) in enumerate(
+            (
+                (mod_far, mod_ref),
+                (hidden_far, hidden_ref),
+                (head_far, head_ref),
+                (cmid_far, cmid_ref),
+                (cin_far, cin_ref),
+                (patch_far, patch_ref),
+                (text_far, text_ref),
+            )
+        )
+    ]
+    for load in loads:
+        load.start()
+
     barrier = pltpu.get_barrier_semaphore()
 
     def greet(to_dp, to_mp):
@@ -172,6 +207,9 @@
         greet(lax.rem(dp + d, NDP), mp)
 
     greet(other_dp, other_mp)
+
+    for load in loads[0:4]:
+        load.wait()
 
     modulation = mod_ref[step_ref[0]].astype(F32)
     across = lax.broadcasted_iota(jnp.int32, (FEAT, FEAT), 1)
@@ -191,7 +229,7 @@
             modulated[:, columns] = block
             halves.append(dot(head_ref[...], block))
         total = jnp.concatenate(halves, axis=0).T
-        parts_out[pl.ds(n * 8, 8)] = total.astype(BF16).reshape(8, Q, 128)
+        parts_out[n] = total.astype(BF16).reshape(8, Q, 128)
 
     @pl.loop(0, 18)
     def _(t):
@@ -202,10 +240,11 @@
 
     send(sibling_out, sibling_in, sib_sems.at[0], sib_sems.at[1], sibling, mp)
 
-    @pl.loop(1, NMP)
-    def _(d):
-        to = lax.rem(mp + d, NMP)
-        send(parts_out.at[to], parts_in.at[NMP - 1 - d], parts_sems.at[0], parts_sems.at[1], dp, to)
+    for dk in (2, 1, 3, 0):
+        for n, (dz, dy) in enumerate(NEAR):
+            to = near(dz, dy)
+            block = parts_out.at[lax.rem(to // 8 + dk, 4), lax.rem(to, 8)]
+            send(block, parts_in.at[dk, n], parts_send, parts_recv.at[dk], dp, to)
 
     wait(sibling_in, sib_sems.at[1])
 
@@ -222,20 +261,26 @@
         high = jnp.where(core == 0, other, own)
         weights[t, own_rows, :] = jnp.concatenate([low[0:24], high[0:24]], axis=0).astype(BF16)
 
-    def piece(i, j, c):
-        return weights.at[pl.ds(3 * (2 * i + c), 3), shard_rows(j), :]
-
-    def pass_on(i, j, kind, to_dp, to_mp):
-        block = piece(i, j, core)
-        send(block, block, w_send, w_recv.at[kind, i], to_dp, to_mp)
-
-    def hand_over(i, j, kind):
-        block = piece(i, j, core)
-        send(block, block, w_send, s_recv.at[kind, i], sibling, mp)
-
-    def arrived(i, j, kind):
-        wait(piece(i, j, core), w_recv.at[kind, i])
-        hand_over(i, j, kind)
+    solo, lent = 1 + y_lo, 2 - y_lo
+    SOLO, LENT = 1, 2
+    index = (0, solo, lent)
+
+    def piece(slot, j, c):
+        return weights.at[pl.ds(3 * (2 * index[slot] + c), 3), shard_rows(j), :]
+
+    def pass_on(slot, j, kind, to_dp, to_mp, to_slot=None):
+        block = piece(slot, j, core)
+        to_slot = slot if to_slot is None else to_slot
+        send(block, block, w_send, w_recv.at[kind, to_slot], to_dp, to_mp)
+
+    def arrived(slot, j, kind):
+        wait(piece(slot, j, core), w_recv.at[kind, slot])
+
+    def hand_over(slot, j, kind):
+        if slot == SOLO and kind != BESIDE:
+            pass_on(slot, j, kind, dp, mp + 1 - 2 * y_lo, LENT)
+        block = piece(slot, j, core)
+        send(block, block, w_send, s_recv.at[kind, slot], sibling, mp)
 
     BESIDE, LEFT, RIGHT, LEFT2, RIGHT2, FAR, FAR2 = range(7)
     own = mine + x
@@ -248,10 +293,38 @@
         (FAR, mine + far_x),
         (FAR2, beside + far_x),
     )
-    for i in range(3):
-        pass_on(i, own, BESIDE, other_dp, other_mp)
-        pass_on(i, own, LEFT, right, mp)
-        pass_on(i, own, RIGHT, left, mp)
+    pass_on(LENT, own, BESIDE, other_dp, other_mp, SOLO)
+    pass_on(SOLO, own, LEFT, right, mp)
+    pass_on(SOLO, own, RIGHT, left, mp)
+
+    def near_sum(dk):
+        wait(parts_in.at[dk], parts_recv.at[dk])
+        total = parts_out[lax.rem(block_row + dk, 4), block_column].astype(F32)
+        for n in range(len(NEAR)):
+            total = total + parts_in[dk, n].astype(F32)
+        return total
+
+    for dk in (2, 1, 3):
+        sums_out[dk - 1] = near_sum(dk).astype(BF16)
+        send(sums_out.at[dk - 1], sums_in.at[dk - 1], sums_sems.at[0], sums_sems.at[1], dp, far(dk))
+    own_sum[...] = near_sum(0)
+
+    for load in loads[4:7]:
+        load.wait()
+
+    arrived(SOLO, beside + x, BESIDE)
+    pass_on(SOLO, beside + x, LEFT2, right, mp)
+    pass_on(SOLO, beside + x, RIGHT2, left, mp)
+    pass_on(0, own, BESIDE, other_dp, other_mp)
+    pass_on(0, own, LEFT, right, mp)
+    pass_on(0, own, RIGHT, left, mp)
+    hand_over(SOLO, beside + x, BESIDE)
+    arrived(SOLO, mine + left_x, LEFT)
+    pass_on(SOLO, mine + left_x, FAR, right, mp)
+    hand_over(SOLO, mine + left_x, LEFT)
+    arrived(SOLO, mine + right_x, RIGHT)
+    hand_over(SOLO, mine + right_x, RIGHT)
+    pass_on(SOLO, own, BESIDE, other_dp, other_mp, LENT)
 
     first_weight[...] = jnp.zeros_like(first_weight)
     for a in range(2):
@@ -269,23 +342,33 @@
         head_wide[f, :, f * 64 : (f + 1) * 64] = head_ref[...].astype(F32).T.astype(BF16)
     place[...] = window_placement()
 
-    for i in range(3):
-        arrived(i, beside + x, BESIDE)
-        pass_on(i, beside + x, LEFT2, right, mp)
-        pass_on(i, beside + x, RIGHT2, left, mp)
-    for i in range(3):
-        arrived(i, mine + left_x, LEFT)
-        pass_on(i, mine + left_x, FAR, right, mp)
-        arrived(i, mine + right_x, RIGHT)
-
-    wait(parts_in, parts_sems.at[1])
-    latent = parts_out[mp].astype(F32)
-    for s in range(NMP - 1):
-        latent = latent + parts_in[s].astype(F32)
+    arrived(SOLO, beside + right_x, RIGHT2)
+    pass_on(SOLO, beside + right_x, FAR2, left, mp)
+    hand_over(SOLO, beside + right_x, RIGHT2)
+    arrived(SOLO, beside + left_x, LEFT2)
+    hand_over(SOLO, beside + left_x, LEFT2)
+    arrived(0, beside + x, BESIDE)
+    pass_on(0, beside + x, LEFT2, right, mp)
+    pass_on(0, beside + x, RIGHT2, left, mp)
+    hand_over(0, beside + x, BESIDE)
+
+    wait(sums_in, sums_sems.at[1])
+    latent = own_sum[...]
+    for n in range(3):
+        latent = latent + sums_in[n].astype(F32)
     latents[2] = latent.astype(BF16)
     for n, d in enumerate((-2, -1, 1, 2)):
         to = lax.rem(mp + d + NMP, NMP)
         send(latents.at[2], latents.at[2 - d], halo_send.at[n], halo_recv.at[n], dp, to)
+
+    arrived(0, mine + left_x, LEFT)
+    pass_on(0, mine + left_x, FAR, right, mp)
+    hand_over(0, mine + left_x, LEFT)
+    arrived(0, mine + right_x, RIGHT)
+    hand_over(0, mine + right_x, RIGHT)
+    arrived(SOLO, mine + far_x, FAR)
+    hand_over(SOLO, mine + far_x, FAR)
+
     for n, d in enumerate((-2, -1, 1, 2)):
         wait(latents.at[2 - d], halo_recv.at[n])
 
@@ -310,17 +393,27 @@
             slope_first[f, :, j * Q : (j + 1) * Q, :] = slope[2 * Q : 6 * Q].reshape(4, Q, CH)
         spread(field, f, columns[0], columns[1], False)
 
+    arrived(SOLO, beside + far_x, FAR2)
+    hand_over(SOLO, beside + far_x, FAR2)
+    arrived(0, beside + right_x, RIGHT2)
+    pass_on(0, beside + right_x, FAR2, left, mp)
+    hand_over(0, beside + right_x, RIGHT2)
+    arrived(0, beside + left_x, LEFT2)
+    hand_over(0, beside + left_x, LEFT2)
+    arrived(LENT, beside + x, BESIDE)
+    hand_over(LENT, beside + x, BESIDE)
+    arrived(0, mine + far_x, FAR)
+    hand_over(0, mine + far_x, FAR)
+    arrived(0, beside + far_x, FAR2)
+    hand_over(0, beside + far_x, FAR2)
+    for kind, j in kinds[1:]:
+        arrived(LENT, j, kind)
+        hand_over(LENT, j, kind)
+
     for i in range(3):
-        arrived(i, beside + left_x, LEFT2)
-        arrived(i, beside + right_x, RIGHT2)
-        pass_on(i, beside + right_x, FAR2, left, mp)
-    for i in range(3):
-        arrived(i, mine + far_x, FAR)
-        arrived(i, beside + far_x, FAR2)
-
-    for i in range(3):
-        for kind, j in kinds:
-            wait(piece(i, j, 1 - core), s_recv.at[kind, i])
+        for slot in ((0,), (SOLO, LENT), ())[i]:
+            for kind, j in kinds:
+                wait(piece(slot, j, 1 - core), s_recv.at[kind, slot])
         for g in (2 * i, 2 * i + 1):
             a, b = g // 3, g % 3
             weight = weights[3 * g : 3 * g + 3].reshape(3 * CH, CH)
@@ -332,13 +425,10 @@
                 else:
                     second[f] = second[f] + value
 
-    pooled_all[mp] = jnp.zeros((8, 128), F32)
     for f in range(2):
         value = second[f, 128:256]
         decoded = (value * sigmoid(value)).astype(BF16).astype(F32)
-        sums = jnp.sum(decoded, axis=0, keepdims=True)
-        for n in range(3):
-            pooled_all[mp, 3 * f + n : 3 * f + n + 1, :] = sums[:, n * 128 : (n + 1) * 128]
+        pooled_all[mp, :, f * CH : (f + 1) * CH] = jnp.sum(decoded, axis=0, keepdims=True)
 
     @pl.loop(1, NMP)
     def _(d):
@@ -358,8 +448,7 @@
     for s in range(1, NMP):
         sums = sums + pooled_all[s]
     sums = sums * (1.0 / CELLS)
-    frames = [jnp.concatenate([sums[3 * f + n : 3 * f + n + 1] for n in range(3)], axis=1) for f in range(2)]
-    pooled = jnp.concatenate(frames, axis=0)
+    pooled = jnp.concatenate([sums[:, 0:CH], sums[:, CH : 2 * CH]], axis=0)
     rows = dot(three_parts(pooled), patch_ref[...])
     embedded = rows[0:2] + rows[2:4] + rows[4:6]
     text = text_ref[...]
@@ -404,79 +493,61 @@
                         term = taps[f + 1 - a][at : at + Q, lane : lane + 16]
                         total = term if total is None else total + term
                 blocks.append(total)
-    grads[mp] = jnp.concatenate(blocks, axis=1).astype(BF16)
-
-    @pl.loop(1, NMP)
-    def _(d):
-        to = lax.rem(mp + d, NMP)
-        send(grads.at[mp], grads.at[mp], grad_sems.at[0], grad_sems.at[1], dp, to)
-
-    wait(grads.at[pl.ds(0, NMP - 1)], grad_sems.at[1])
+    grads[block_row, block_column] = jnp.concatenate(blocks, axis=1).astype(BF16)
+
+    def spread_near(row):
+        block = grads.at[row, block_column]
+        for dz, dy in NEAR:
+            send(block, block, near_sems.at[0], near_sems.at[1], dp, near(dz, dy))
+
+    for dk in (2, 1, 3):
+        block = grads.at[block_row, block_column]
+        send(block, block, far_send, far_recv.at[dk - 1], dp, far(dk))
+    spread_near(block_row)
+    for dk in (1, 3, 2):
+        row = lax.rem(block_row + 4 - dk, 4)
+        wait(grads.at[row, block_column], far_recv.at[dk - 1])
+        spread_near(row)
+    wait(grads.at[:, pl.ds(0, 7)], near_sems.at[1])
     token_grad = grads[...].reshape(NMP * Q, 128)
 
     early = dot(modulated[:, 0:1024], token_grad).T
     late = dot(modulated[:, 1024:2048], token_grad).T
-    head_out[...] = early[0:64] + late[64:128]
-
-    @pl.loop(0, OWNERS)
-    def _(c):
-        @pl.when(c != dp)
-        def _():
-            block = head_out.at[pl.ds(pl.multiple_of(8 * c, 8), 8)]
-            send(block, head_in.at[dp], head_sems.at[0], head_sems.at[1], c, mp)
+    part = early[0:64] + late[64:128]
+    rest = [part[r * 16 : (r + 1) * 16, 128:FEAT] for r in range(4)]
+    head_in[dp, 0:64, :] = part[:, 0:128].astype(BF16)
+    head_in[dp, 64:80, :] = jnp.concatenate(rest, axis=1).astype(BF16)
+
+    @pl.loop(1, NDP)
+    def _(d):
+        block = head_in.at[dp]
+        send(block, block, head_sems.at[0], head_sems.at[1], lax.rem(dp + d, NDP), mp)
 
     def hidden_part(f):
         value = dot(head_wide[f], grads[...].reshape(NMP * Q, 128), NT) * gain
-        hidden_out[:, f * 1024 : (f + 1) * 1024] = value.astype(BF16)
-        columns = pl.ds(f * 1024, 1024)
-        pltpu.make_async_copy(
-            hidden_out.at[:, columns], hidden_grad_ref.at[:, columns], out_sem.at[f]
-        ).start()
+        hidden_grad_ref[:, f * 1024 : (f + 1) * 1024] = value.astype(BF16)
 
     hidden_part(0)
-    own_block = pl.ds(pl.multiple_of(8 * jnp.minimum(dp, OWNERS - 1), 8), 8)
-
-    @pl.when(dp < OWNERS)
-    def _():
-        head_in[dp] = head_out[own_block, :]
-        wait(head_in.at[pl.ds(0, NDP - 1)], head_sems.at[1])
-        total = head_in[0]
-        for s in range(1, NDP):
-            total = total + head_in[s]
-        head_sum[own_block, :] = total
-
-        @pl.loop(1, NDP)
-        def _(d):
-            block = head_sum.at[own_block]
-            send(block, block, total_sems.at[0], total_sems.at[1], lax.rem(dp + d, NDP), mp)
-
     hidden_part(1)
 
-    @pl.when(dp < OWNERS)
-    def _():
-        wait(head_sum.at[pl.ds(0, 8 * (OWNERS - 1))], total_sems.at[1])
-        wait(head_in.at[pl.ds(0, NDP - 1)], total_sems.at[0])
-        wait(head_out.at[pl.ds(0, 8 * (OWNERS - 1))], head_sems.at[0])
-
-    @pl.when(dp >= OWNERS)
-    def _():
-        wait(head_sum, total_sems.at[1])
-        wait(head_out, head_sems.at[0])
-
-    head_grad_ref[...] = head_sum[...]
-
+    wait(head_in.at[pl.ds(0, NDP - 1)], head_sems.at[1])
+    total = head_in[0].astype(F32)
+    for s in range(1, NDP):
+        total = total + head_in[s].astype(F32)
+    head_grad_ref[:, 0:128] = total[0:64]
+    for r in range(4):
+        head_grad_ref[r * 16 : (r + 1) * 16, 128:FEAT] = total[64:80, r * 32 : (r + 1) * 32]
+
+    wait(head_in.at[pl.ds(0, NDP - 1)], head_sems.at[0])
     wait(sibling_out, sib_sems.at[0])
-    wait(parts_in, parts_sems.at[0])
+    wait(parts_in, parts_send)
     for n in range(4):
         wait(latents.at[2], halo_send.at[n])
     wait(weights.at[:, pl.ds(0, 7 * SHARD), :], w_send)
     wait(pooled_all.at[pl.ds(0, NMP - 1)], pool_sems.at[0])
-    wait(grads.at[pl.ds(0, NMP - 1)], grad_sems.at[0])
-    for f in range(2):
-        columns = pl.ds(f * 1024, 1024)
-        pltpu.make_async_copy(
-            hidden_out.at[:, columns], hidden_grad_ref.at[:, columns], out_sem.at[f]
-        ).wait()
+    wait(sums_in, sums_sems.at[0])
+    wait(grads.at[0, pl.ds(0, 3)], far_send)
+    wait(grads.at[:, pl.ds(0, 7)], near_sems.at[0])
 
 
 def body(hidden, mod_table, timestep, head_weight, conv_in, conv_mid, patch_weight, text_emb):
@@ -485,18 +556,28 @@
     reward, head_grad, hidden_grad = pl.pallas_call(
         kernel,
         out_shape=(
-            jax.ShapeDtypeStruct((1, 128), F32),
-            jax.ShapeDtypeStruct((64, FEAT), F32),
-            jax.ShapeDtypeStruct((FEAT, 2048), BF16),
+            pltpu.VMEM((1, 128), F32),
+            pltpu.VMEM((64, FEAT), F32),
+            pltpu.VMEM((FEAT, 2048), BF16),
         ),
-        in_specs=[pl.BlockSpec(memory_space=pltpu.SMEM)] + [vmem] * 7,
-        out_specs=(vmem, vmem, pl.BlockSpec(memory_space=pl.ANY)),
+        in_specs=[pl.BlockSpec(memory_space=pltpu.SMEM)] + [pl.BlockSpec(memory_space=pltpu.HBM)] * 7,
+        out_specs=(vmem, vmem, vmem),
         scratch_shapes=[
+            pltpu.VMEM((FEAT, 2048), BF16),
+            pltpu.VMEM((50, 2, FEAT), BF16),
+            pltpu.VMEM((64, FEAT), BF16),
+            pltpu.VMEM((27, 24, CH), BF16),
+            pltpu.VMEM((27, C, CH), BF16),
+            pltpu.VMEM((CH, EMB), BF16),
+            pltpu.VMEM((1, EMB), F32),
             pltpu.VMEM((FEAT, 2048), BF16),
             pltpu.VMEM((2, FEAT, 128), BF16),
             pltpu.VMEM((384, 512), BF16),
-            pltpu.VMEM((NMP, Q, 128), BF16),
-            pltpu.VMEM((NMP - 1, Q, 128), BF16),
+            pltpu.VMEM((4, 8, Q, 128), BF16),
+            pltpu.VMEM((4, 7, Q, 128), BF16),
+            pltpu.VMEM((3, Q, 128), BF16),
+            pltpu.VMEM((3, Q, 128), BF16),
+            pltpu.VMEM((Q, 128), F32),
             pltpu.VMEM((5, Q, 128), BF16),
             pltpu.VMEM((2, 10, Q, 128), BF16),
             pltpu.VMEM((384, 2 * CH), BF16),
@@ -509,13 +590,12 @@
             pltpu.VMEM((18, CH, CH), BF16),
             pltpu.VMEM((18, 32, CH), BF16),
             pltpu.VMEM((18, 32, CH), BF16),
-            pltpu.VMEM((NMP, 8, 128), F32),
-            pltpu.VMEM((NMP, Q, 128), BF16),
-            pltpu.VMEM((FEAT, 2048), BF16),
-            pltpu.VMEM((64, FEAT), F32),
-            pltpu.VMEM((NDP, 8, FEAT), F32),
-            pltpu.VMEM((64, FEAT), F32),
+            pltpu.VMEM((NMP, 1, 2 * CH), F32),
+            pltpu.VMEM((4, 8, Q, 128), BF16),
+            pltpu.VMEM((NDP, 80, 128), BF16),
             dma((2,)),
+            dma,
+            dma((4,)),
             dma((2,)),
             dma((4,)),
             dma((4,)),
@@ -523,10 +603,11 @@
             dma((7, 3)),
             dma((7, 3)),
             dma((2,)),
+            dma,
+            dma((3,)),
             dma((2,)),
             dma((2,)),
-            dma((2,)),
-            dma((2,)),
+            dma((7,)),
         ],
         compiler_params=pltpu.CompilerParams(
             collective_id=0, has_side_effects=True, vmem_limit_bytes=48 * 1024 * 1024
@@ -534,13 +615,18 @@
         name="guided_step",
     )(
         timestep,
-        hidden.T,
-        mod_table,
-        head_weight.T,
-        jnp.transpose(conv_in, (1, 0, 2)),
-        jnp.transpose(conv_mid, (1, 0, 2)),
-        patch_weight,
-        text_emb,
+        *(
+            pltpu.with_memory_space_constraint(operand, pltpu.HBM)
+            for operand in (
+                hidden.T,
+                mod_table,
+                head_weight.T,
+                jnp.transpose(conv_mid, (1, 0, 2)),
+                jnp.transpose(conv_in, (1, 0, 2)),
+                patch_weight,
+                text_emb,
+            )
+        ),
     )
     return (reward[0, 0:1], head_grad.T, hidden_grad.T)
 

time: 104 us -> 84.6 us (0.81)
  Pallas kernels: 93.2 us -> 80.5 us
  local copies, waits for them, and re-layouts: 7.93 us -> 1.47 us
    pallas_call x1, Pallas kernels: 93.2 us -> 80.5 us  [body(): pl.pallas_call(kernel, out_shape=(pltpu.VMEM((1, 128), F32), pltpu.VMEM((...]
    unnamed x16 -> x2, local copies, waits for them, and re-layouts: 7.93 us -> 1.47 us
where the time goes in v2:
time: 84.6 us; the launch traced here: 84.4 us
  Pallas kernels  80.5 us (95%)
  between operations  2.45 us (3%)
  local copies, waits for them, and re-layouts  1.47 us (2%)
    pallas_call x1, Pallas kernels, body(): pl.pallas_call(kernel, out_shape=(pltpu.VMEM((1, 128), F32), pltpu.VMEM((...  80.5 us

profile of v2, /device:TPU:1, one launch (start us, length us, event | category | flops | bytes accessed | tf_op | source)
XLA Modules:
  0.0 84.4 jit_solution(3926773409564976163)
XLA Ops:
  1.3 80.5 %guided_step.1 = (f32[1,128]{1,0:T(1,128)S(1)}, f32[64,160]{1,0:T(8,128)S(1)}, bf16[160,2048]{1,0:T(8,128)(2,1)S(1)}) custom-call(s32[1]{0:T(128)S(6)} %copy.16.step_ref, bf16[160,2048]{1,0:T(8,128)(2,1)} %bitcast.11, bf16[50,2,160]{2,1,0:T(2,128)(2,1)} %mod_far.1, bf16[64,160]{1,0:T(8,128)(2,1)} %bitcast.14, bf16[27,24,384]{2,1,0:T(8,128)(2,1)} %bitcast.12, ...), custom_call_target="tpu_custom_call" | custom-call | tf_op jit(solution)/shard_map/guided_step/pallas_call | solution.py:556
  81.8 0.6 copy.14
  82.4 0.8 copy.15

commit v3 on v2

--- a/solution.py
+++ b/solution.py
@@ -178,10 +178,10 @@
         pltpu.make_async_copy(far, near, in_sems.at[n])
         for n, (far, near) in enumerate(
             (
+                (cmid_far, cmid_ref),
                 (mod_far, mod_ref),
                 (hidden_far, hidden_ref),
                 (head_far, head_ref),
-                (cmid_far, cmid_ref),
                 (cin_far, cin_ref),
                 (patch_far, patch_ref),
                 (text_far, text_ref),
@@ -208,7 +208,18 @@
 
     greet(other_dp, other_mp)
 
-    for load in loads[0:4]:
+    loads[0].wait()
+
+    @pl.loop(0, 18)
+    def _(t):
+        own = cmid_ref[t + 9].astype(F32)
+        sibling_out[t] = jnp.concatenate([own, jnp.zeros((8, CH), F32)], axis=0).astype(BF16)
+
+    pl.semaphore_wait(barrier, NMP - 1 + NDP - 1 + 1)
+
+    send(sibling_out, sibling_in, sib_sems.at[0], sib_sems.at[1], sibling, mp)
+
+    for load in loads[1:4]:
         load.wait()
 
     modulation = mod_ref[step_ref[0]].astype(F32)
@@ -231,15 +242,6 @@
         total = jnp.concatenate(halves, axis=0).T
         parts_out[n] = total.astype(BF16).reshape(8, Q, 128)
 
-    @pl.loop(0, 18)
-    def _(t):
-        own = cmid_ref[t + 9].astype(F32)
-        sibling_out[t] = jnp.concatenate([own, jnp.zeros((8, CH), F32)], axis=0).astype(BF16)
-
-    pl.semaphore_wait(barrier, NMP - 1 + NDP - 1 + 1)
-
-    send(sibling_out, sibling_in, sib_sems.at[0], sib_sems.at[1], sibling, mp)
-
     for dk in (2, 1, 3, 0):
         for n, (dz, dy) in enumerate(NEAR):
             to = near(dz, dy)
@@ -279,6 +281,8 @@
     def hand_over(slot, j, kind):
         if slot == SOLO and kind != BESIDE:
             pass_on(slot, j, kind, dp, mp + 1 - 2 * y_lo, LENT)
+        if slot == 0 and kind in (LEFT, RIGHT, FAR):
+            pass_on(slot, j, {LEFT: LEFT2, RIGHT: RIGHT2, FAR: FAR2}[kind], other_dp, other_mp)
         block = piece(slot, j, core)
         send(block, block, w_send, s_recv.at[kind, slot], sibling, mp)
 
@@ -296,35 +300,11 @@
     pass_on(LENT, own, BESIDE, other_dp, other_mp, SOLO)
     pass_on(SOLO, own, LEFT, right, mp)
     pass_on(SOLO, own, RIGHT, left, mp)
-
-    def near_sum(dk):
-        wait(parts_in.at[dk], parts_recv.at[dk])
-        total = parts_out[lax.rem(block_row + dk, 4), block_column].astype(F32)
-        for n in range(len(NEAR)):
-            total = total + parts_in[dk, n].astype(F32)
-        return total
-
-    for dk in (2, 1, 3):
-        sums_out[dk - 1] = near_sum(dk).astype(BF16)
-        send(sums_out.at[dk - 1], sums_in.at[dk - 1], sums_sems.at[0], sums_sems.at[1], dp, far(dk))
-    own_sum[...] = near_sum(0)
+    pass_on(0, own, LEFT, right, mp)
+    pass_on(0, own, RIGHT, left, mp)
 
     for load in loads[4:7]:
         load.wait()
-
-    arrived(SOLO, beside + x, BESIDE)
-    pass_on(SOLO, beside + x, LEFT2, right, mp)
-    pass_on(SOLO, beside + x, RIGHT2, left, mp)
-    pass_on(0, own, BESIDE, other_dp, other_mp)
-    pass_on(0, own, LEFT, right, mp)
-    pass_on(0, own, RIGHT, left, mp)
-    hand_over(SOLO, beside + x, BESIDE)
-    arrived(SOLO, mine + left_x, LEFT)
-    pass_on(SOLO, mine + left_x, FAR, right, mp)
-    hand_over(SOLO, mine + left_x, LEFT)
-    arrived(SOLO, mine + right_x, RIGHT)
-    hand_over(SOLO, mine + right_x, RIGHT)
-    pass_on(SOLO, own, BESIDE, other_dp, other_mp, LENT)
 
     first_weight[...] = jnp.zeros_like(first_weight)
     for a in range(2):
@@ -342,15 +322,40 @@
         head_wide[f, :, f * 64 : (f + 1) * 64] = head_ref[...].astype(F32).T.astype(BF16)
     place[...] = window_placement()
 
+    def near_sum(dk):
+        wait(parts_in.at[dk], parts_recv.at[dk])
+        total = parts_out[lax.rem(block_row + dk, 4), block_column].astype(F32)
+        for n in range(len(NEAR)):
+            total = total + parts_in[dk, n].astype(F32)
+        return total
+
+    for dk in (2, 1, 3):
+        sums_out[dk - 1] = near_sum(dk).astype(BF16)
+        send(sums_out.at[dk - 1], sums_in.at[dk - 1], sums_sems.at[0], sums_sems.at[1], dp, far(dk))
+    own_sum[...] = near_sum(0)
+
+    arrived(SOLO, beside + x, BESIDE)
+    pass_on(SOLO, beside + x, LEFT2, right, mp)
+    pass_on(SOLO, beside + x, RIGHT2, left, mp)
+    hand_over(SOLO, beside + x, BESIDE)
+    arrived(SOLO, mine + left_x, LEFT)
+    pass_on(SOLO, mine + left_x, FAR, right, mp)
+    hand_over(SOLO, mine + left_x, LEFT)
+    arrived(SOLO, mine + right_x, RIGHT)
+    hand_over(SOLO, mine + right_x, RIGHT)
+    pass_on(0, own, BESIDE, other_dp, other_mp)
+    pass_on(SOLO, own, BESIDE, other_dp, other_mp, LENT)
+    arrived(0, mine + left_x, LEFT)
+    pass_on(0, mine + left_x, FAR, right, mp)
+    hand_over(0, mine + left_x, LEFT)
+    arrived(0, mine + right_x, RIGHT)
+    hand_over(0, mine + right_x, RIGHT)
+
     arrived(SOLO, beside + right_x, RIGHT2)
     pass_on(SOLO, beside + right_x, FAR2, left, mp)
     hand_over(SOLO, beside + right_x, RIGHT2)
     arrived(SOLO, beside + left_x, LEFT2)
     hand_over(SOLO, beside + left_x, LEFT2)
-    arrived(0, beside + x, BESIDE)
-    pass_on(0, beside + x, LEFT2, right, mp)
-    pass_on(0, beside + x, RIGHT2, left, mp)
-    hand_over(0, beside + x, BESIDE)
 
     wait(sums_in, sums_sems.at[1])
     latent = own_sum[...]
@@ -361,13 +366,16 @@
         to = lax.rem(mp + d + NMP, NMP)
         send(latents.at[2], latents.at[2 - d], halo_send.at[n], halo_recv.at[n], dp, to)
 
-    arrived(0, mine + left_x, LEFT)
-    pass_on(0, mine + left_x, FAR, right, mp)
-    hand_over(0, mine + left_x, LEFT)
-    arrived(0, mine + right_x, RIGHT)
-    hand_over(0, mine + right_x, RIGHT)
     arrived(SOLO, mine + far_x, FAR)
     hand_over(SOLO, mine + far_x, FAR)
+    arrived(0, mine + far_x, FAR)
+    hand_over(0, mine + far_x, FAR)
+    arrived(SOLO, beside + far_x, FAR2)
+    hand_over(SOLO, beside + far_x, FAR2)
+    arrived(0, beside + x, BESIDE)
+    hand_over(0, beside + x, BESIDE)
+    arrived(LENT, beside + x, BESIDE)
+    hand_over(LENT, beside + x, BESIDE)
 
     for n, d in enumerate((-2, -1, 1, 2)):
         wait(latents.at[2 - d], halo_recv.at[n])
@@ -393,37 +401,37 @@
             slope_first[f, :, j * Q : (j + 1) * Q, :] = slope[2 * Q : 6 * Q].reshape(4, Q, CH)
         spread(field, f, columns[0], columns[1], False)
 
-    arrived(SOLO, beside + far_x, FAR2)
-    hand_over(SOLO, beside + far_x, FAR2)
-    arrived(0, beside + right_x, RIGHT2)
-    pass_on(0, beside + right_x, FAR2, left, mp)
-    hand_over(0, beside + right_x, RIGHT2)
-    arrived(0, beside + left_x, LEFT2)
-    hand_over(0, beside + left_x, LEFT2)
-    arrived(LENT, beside + x, BESIDE)
-    hand_over(LENT, beside + x, BESIDE)
-    arrived(0, mine + far_x, FAR)
-    hand_over(0, mine + far_x, FAR)
-    arrived(0, beside + far_x, FAR2)
-    hand_over(0, beside + far_x, FAR2)
     for kind, j in kinds[1:]:
+        if kind in (LEFT2, RIGHT2, FAR2):
+            arrived(0, j, kind)
+            hand_over(0, j, kind)
         arrived(LENT, j, kind)
         hand_over(LENT, j, kind)
-
-    for i in range(3):
-        for slot in ((0,), (SOLO, LENT), ())[i]:
-            for kind, j in kinds:
-                wait(piece(slot, j, 1 - core), s_recv.at[kind, slot])
-        for g in (2 * i, 2 * i + 1):
-            a, b = g // 3, g % 3
-            weight = weights[3 * g : 3 * g + 3].reshape(3 * CH, CH)
-            for f in range(1 - a, 2):
-                source = field[f + a - 1, b : b + 6].reshape(6 * 64, 3 * CH)
-                value = dot(source, weight)
-                if (g, f) in ((0, 1), (3, 0)):
-                    second[f] = value
-                else:
-                    second[f] = second[f] + value
+    for slot in range(3):
+        for kind, j in kinds:
+            wait(piece(slot, j, 1 - core), s_recv.at[kind, slot])
+
+    def tap(a, b):
+        at = 9 * a + 3 * b
+        return weights[at : at + 3].reshape(3 * CH, CH)
+
+    def middle(starts):
+        early, late = None, None
+        for b in range(3):
+            both = jnp.concatenate([tap(1, b), tap(0, b)], axis=1)
+            sources = [
+                jnp.concatenate([field[f, r + b : r + b + 2].reshape(128, 3 * CH) for r in starts], axis=0)
+                for f in range(2)
+            ]
+            terms = dot(sources[0], both), dot(sources[1], tap(1, b))
+            early = terms[0] if early is None else early + terms[0]
+            late = terms[1] if late is None else late + terms[1]
+        late = late + early[:, CH : 2 * CH]
+        for n, r in enumerate(starts):
+            second[0, r * 64 : r * 64 + 128] = early[n * 128 : (n + 1) * 128, 0:CH]
+            second[1, r * 64 : r * 64 + 128] = late[n * 128 : (n + 1) * 128]
+
+    middle((2,))
 
     for f in range(2):
         value = second[f, 128:256]
@@ -435,6 +443,7 @@
         to = lax.rem(mp + d, NMP)
         send(pooled_all.at[mp], pooled_all.at[mp], pool_sems.at[0], pool_sems.at[1], dp, to)
 
+    middle((0, 4))
     row = lax.broadcasted_iota(jnp.int32, (6 * 64, 1), 0) // 64 + 2 * mp - 2
     inside = jnp.where((row >= 0) & (row < 2 * NMP), 1.0, 0.0)
     for f in range(2):
@@ -466,14 +475,18 @@
         spread(back_field, f, grad[:, 0:Q].reshape(6 * Q, CH), grad[:, Q:].reshape(6 * Q, CH), True)
     row = lax.broadcasted_iota(jnp.int32, (4 * 64, 1), 0) // 64 + 2 * mp - 1
     inside = jnp.where((row >= 0) & (row < 2 * NMP), 1.0, 0.0)
+    late, early = None, None
+    for b in range(3):
+        sources = [back_field[f, 2 - b : 6 - b].reshape(4 * 64, 3 * CH) for f in range(2)]
+        both = [
+            jnp.concatenate([weights[9 * a + 3 * b + c] for c in range(3)], axis=1) for a in range(2)
+        ]
+        terms = dot(sources[1], jnp.concatenate([both[1], both[0]], axis=0), NT), dot(sources[0], both[1], NT)
+        late = terms[0] if late is None else late + terms[0]
+        early = terms[1] if early is None else early + terms[1]
+    grad_field = (early + late[:, CH : 2 * CH], late[:, 0:CH])
     for f in range(2):
-        total = None
-        for a in range(f, 2):
-            for b in range(3):
-                source = back_field[f + 1 - a, 2 - b : 6 - b].reshape(4 * 64, 3 * CH)
-                for c in range(3):
-                    term = dot(source[:, c * CH : (c + 1) * CH], weights[9 * a + 3 * b + c], NT)
-                    total = term if total is None else total + term
+        total = grad_field[f]
         total = total * slope_first[f].reshape(4 * 64, CH) * inside
         total = total.reshape(4, 64, CH)
         spread(back_first, f, total[:, 0:Q].reshape(4 * Q, CH), total[:, Q:].reshape(4 * Q, CH), True)

time: 84.6 us -> 79.7 us (0.942)
  Pallas kernels: 80.5 us -> 75.7 us
    pallas_call x1, Pallas kernels: 80.5 us -> 75.7 us  [body(): pl.pallas_call(kernel, out_shape=(pltpu.VMEM((1, 128), F32), pltpu.VMEM((...]
where the time goes in v3:
time: 79.7 us; the launch traced here: 79.6 us
  Pallas kernels  75.7 us (95%)
  between operations  2.45 us (3%)
  local copies, waits for them, and re-layouts  1.47 us (2%)
    pallas_call x1, Pallas kernels, body(): pl.pallas_call(kernel, out_shape=(pltpu.VMEM((1, 128), F32), pltpu.VMEM((...  75.7 us

profile of v3, /device:TPU:1, one launch (start us, length us, event | category | flops | bytes accessed | tf_op | source)
XLA Modules:
  0.0 79.6 jit_solution(8894825650415329117)
XLA Ops:
  1.3 75.7 %guided_step.1 = (f32[1,128]{1,0:T(1,128)S(1)}, f32[64,160]{1,0:T(8,128)S(1)}, bf16[160,2048]{1,0:T(8,128)(2,1)S(1)}) custom-call(s32[1]{0:T(128)S(6)} %copy.16.step_ref, bf16[160,2048]{1,0:T(8,128)(2,1)} %bitcast.11, bf16[50,2,160]{2,1,0:T(2,128)(2,1)} %mod_far.1, bf16[64,160]{1,0:T(8,128)(2,1)} %bitcast.14, bf16[27,24,384]{2,1,0:T(8,128)(2,1)} %bitcast.12, ...), custom_call_target="tpu_custom_call" | custom-call | tf_op jit(solution)/shard_map/guided_step/pallas_call | solution.py:569
  76.9 0.6 copy.14
  77.6 0.8 %copy.15 = bf16[2048,160]{0,1:T(8,128)(2,1)} copy(bf16[2048,160]{0,1:T(8,128)(2,1)S(1)} %bitcast.8) | data formatting | bytes 1310720

commit v4 on v3

--- a/solution.py
+++ b/solution.py
@@ -174,6 +174,23 @@
     def wait(ref, sem):
         pltpu.make_async_copy(ref, ref, sem).wait()
 
+    barrier = pltpu.get_barrier_semaphore()
+
+    def greet(to_dp, to_mp):
+        pl.semaphore_signal(
+            barrier, inc=1, device_id=(to_dp, to_mp), device_id_type=pl.DeviceIdType.MESH
+        )
+
+    @pl.loop(1, NMP)
+    def _(d):
+        greet(dp, lax.rem(mp + d, NMP))
+
+    @pl.loop(1, NDP)
+    def _(d):
+        greet(lax.rem(dp + d, NDP), mp)
+
+    greet(other_dp, other_mp)
+
     loads = [
         pltpu.make_async_copy(far, near, in_sems.at[n])
         for n, (far, near) in enumerate(
@@ -191,23 +208,6 @@
     for load in loads:
         load.start()
 
-    barrier = pltpu.get_barrier_semaphore()
-
-    def greet(to_dp, to_mp):
-        pl.semaphore_signal(
-            barrier, inc=1, device_id=(to_dp, to_mp), device_id_type=pl.DeviceIdType.MESH
-        )
-
-    @pl.loop(1, NMP)
-    def _(d):
-        greet(dp, lax.rem(mp + d, NMP))
-
-    @pl.loop(1, NDP)
-    def _(d):
-        greet(lax.rem(dp + d, NDP), mp)
-
-    greet(other_dp, other_mp)
-
     loads[0].wait()
 
     @pl.loop(0, 18)
@@ -263,28 +263,39 @@
         high = jnp.where(core == 0, other, own)
         weights[t, own_rows, :] = jnp.concatenate([low[0:24], high[0:24]], axis=0).astype(BF16)
 
-    solo, lent = 1 + y_lo, 2 - y_lo
+    z_odd = lax.rem(z, 2)
+    solo = 1 + lax.rem(y_lo + z, 2)
+    lent = 3 - solo
     SOLO, LENT = 1, 2
     index = (0, solo, lent)
 
     def piece(slot, j, c):
         return weights.at[pl.ds(3 * (2 * index[slot] + c), 3), shard_rows(j), :]
 
+    def part(slot, j, t):
+        return weights.at[3 * (2 * index[slot] + core) + t, shard_rows(j), :]
+
     def pass_on(slot, j, kind, to_dp, to_mp, to_slot=None):
-        block = piece(slot, j, core)
         to_slot = slot if to_slot is None else to_slot
-        send(block, block, w_send, w_recv.at[kind, to_slot], to_dp, to_mp)
-
-    def arrived(slot, j, kind):
-        wait(piece(slot, j, core), w_recv.at[kind, slot])
-
-    def hand_over(slot, j, kind):
-        if slot == SOLO and kind != BESIDE:
-            pass_on(slot, j, kind, dp, mp + 1 - 2 * y_lo, LENT)
+        for t in range(3):
+            block = part(slot, j, t)
+            send(block, block, w_send, w_recv.at[kind, to_slot, t], to_dp, to_mp)
+
+    def relay(slot, j, kind, *onward):
+        if slot == SOLO and kind in (LEFT, RIGHT, FAR2):
+            onward += ((kind, LENT, dp, mp + 1 - 2 * y_lo),)
+        elif slot == SOLO:
+            onward += ((kind, LENT, dp, mp + 2 - 4 * z_odd),)
         if slot == 0 and kind in (LEFT, RIGHT, FAR):
-            pass_on(slot, j, {LEFT: LEFT2, RIGHT: RIGHT2, FAR: FAR2}[kind], other_dp, other_mp)
-        block = piece(slot, j, core)
-        send(block, block, w_send, s_recv.at[kind, slot], sibling, mp)
+            onward += (({LEFT: LEFT2, RIGHT: RIGHT2, FAR: FAR2}[kind], 0, other_dp, other_mp),)
+        for t in range(3):
+            block = part(slot, j, t)
+            wait(block, w_recv.at[kind, slot, t])
+            for to_kind, to_slot, to_dp, to_mp, *only in onward:
+                if only and t not in only[0]:
+                    continue
+                send(block, block, w_send, w_recv.at[to_kind, to_slot, t], to_dp, to_mp)
+            send(block, block, w_send, s_recv.at[kind, slot], sibling, mp)
 
     BESIDE, LEFT, RIGHT, LEFT2, RIGHT2, FAR, FAR2 = range(7)
     own = mine + x
@@ -334,28 +345,15 @@
         send(sums_out.at[dk - 1], sums_in.at[dk - 1], sums_sems.at[0], sums_sems.at[1], dp, far(dk))
     own_sum[...] = near_sum(0)
 
-    arrived(SOLO, beside + x, BESIDE)
-    pass_on(SOLO, beside + x, LEFT2, right, mp)
-    pass_on(SOLO, beside + x, RIGHT2, left, mp)
-    hand_over(SOLO, beside + x, BESIDE)
-    arrived(SOLO, mine + left_x, LEFT)
-    pass_on(SOLO, mine + left_x, FAR, right, mp)
-    hand_over(SOLO, mine + left_x, LEFT)
-    arrived(SOLO, mine + right_x, RIGHT)
-    hand_over(SOLO, mine + right_x, RIGHT)
+    relay(SOLO, beside + x, BESIDE, (LEFT2, SOLO, right, mp), (RIGHT2, SOLO, left, mp))
+    relay(SOLO, mine + left_x, LEFT, (FAR, SOLO, right, mp))
+    relay(SOLO, mine + right_x, RIGHT)
     pass_on(0, own, BESIDE, other_dp, other_mp)
-    pass_on(SOLO, own, BESIDE, other_dp, other_mp, LENT)
-    arrived(0, mine + left_x, LEFT)
-    pass_on(0, mine + left_x, FAR, right, mp)
-    hand_over(0, mine + left_x, LEFT)
-    arrived(0, mine + right_x, RIGHT)
-    hand_over(0, mine + right_x, RIGHT)
-
-    arrived(SOLO, beside + right_x, RIGHT2)
-    pass_on(SOLO, beside + right_x, FAR2, left, mp)
-    hand_over(SOLO, beside + right_x, RIGHT2)
-    arrived(SOLO, beside + left_x, LEFT2)
-    hand_over(SOLO, beside + left_x, LEFT2)
+    relay(0, mine + left_x, LEFT, (FAR, 0, right, mp, (0, 1)))
+    relay(0, mine + right_x, RIGHT, (FAR, 0, left, mp, (2,)))
+
+    relay(SOLO, beside + right_x, RIGHT2, (FAR2, SOLO, left, mp))
+    relay(SOLO, beside + left_x, LEFT2)
 
     wait(sums_in, sums_sems.at[1])
     latent = own_sum[...]
@@ -366,16 +364,11 @@
         to = lax.rem(mp + d + NMP, NMP)
         send(latents.at[2], latents.at[2 - d], halo_send.at[n], halo_recv.at[n], dp, to)
 
-    arrived(SOLO, mine + far_x, FAR)
-    hand_over(SOLO, mine + far_x, FAR)
-    arrived(0, mine + far_x, FAR)
-    hand_over(0, mine + far_x, FAR)
-    arrived(SOLO, beside + far_x, FAR2)
-    hand_over(SOLO, beside + far_x, FAR2)
-    arrived(0, beside + x, BESIDE)
-    hand_over(0, beside + x, BESIDE)
-    arrived(LENT, beside + x, BESIDE)
-    hand_over(LENT, beside + x, BESIDE)
+    relay(SOLO, mine + far_x, FAR)
+    relay(0, mine + far_x, FAR)
+    relay(SOLO, beside + far_x, FAR2)
+    relay(0, beside + x, BESIDE)
+    relay(LENT, beside + x, BESIDE)
 
     for n, d in enumerate((-2, -1, 1, 2)):
         wait(latents.at[2 - d], halo_recv.at[n])
@@ -403,10 +396,8 @@
 
     for kind, j in kinds[1:]:
         if kind in (LEFT2, RIGHT2, FAR2):
-            arrived(0, j, kind)
-            hand_over(0, j, kind)
-        arrived(LENT, j, kind)
-        hand_over(LENT, j, kind)
+            relay(0, j, kind)
+        relay(LENT, j, kind)
     for slot in range(3):
         for kind, j in kinds:
             wait(piece(slot, j, 1 - core), s_recv.at[kind, slot])
@@ -613,7 +604,7 @@
             dma((4,)),
             dma((4,)),
             dma,
-            dma((7, 3)),
+            dma((7, 3, 3)),
             dma((7, 3)),
             dma((2,)),
             dma,

time: 79.7 us -> 77 us (0.966)
  Pallas kernels: 75.7 us -> 72.9 us
    pallas_call x1, Pallas kernels: 75.7 us -> 72.9 us  [body(): pl.pallas_call(kernel, out_shape=(pltpu.VMEM((1, 128), F32), pltpu.VMEM((...]
where the time goes in v4:
time: 77 us; the launch traced here: 76.8 us
  Pallas kernels  72.9 us (95%)
  between operations  2.45 us (3%)
  local copies, waits for them, and re-layouts  1.47 us (2%)
    pallas_call x1, Pallas kernels, body(): pl.pallas_call(kernel, out_shape=(pltpu.VMEM((1, 128), F32), pltpu.VMEM((...  72.9 us

profile of v4, /device:TPU:1, one launch (start us, length us, event | category | flops | bytes accessed | tf_op | source)
XLA Modules:
  0.0 76.8 jit_solution(15987023544968491032)
XLA Ops:
  1.3 72.9 %guided_step.1 = (f32[1,128]{1,0:T(1,128)S(1)}, f32[64,160]{1,0:T(8,128)S(1)}, bf16[160,2048]{1,0:T(8,128)(2,1)S(1)}) custom-call(s32[1]{0:T(128)S(6)} %copy.16.step_ref, bf16[160,2048]{1,0:T(8,128)(2,1)} %bitcast.11, bf16[50,2,160]{2,1,0:T(2,128)(2,1)} %mod_far.1, bf16[64,160]{1,0:T(8,128)(2,1)} %bitcast.14, bf16[27,24,384]{2,1,0:T(8,128)(2,1)} %bitcast.12, ...), custom_call_target="tpu_custom_call" | custom-call | tf_op jit(solution)/shard_map/guided_step/pallas_call | solution.py:560
  74.2 0.6 copy.14
  74.8 0.8 %copy.15 = bf16[2048,160]{0,1:T(8,128)(2,1)} copy(bf16[2048,160]{0,1:T(8,128)(2,1)S(1)} %bitcast.8) | data formatting | bytes 1310720

commit v5 on v4

--- a/solution.py
+++ b/solution.py
@@ -309,10 +309,10 @@
         (FAR2, beside + far_x),
     )
     pass_on(LENT, own, BESIDE, other_dp, other_mp, SOLO)
+    pass_on(0, own, LEFT, right, mp)
+    pass_on(0, own, RIGHT, left, mp)
     pass_on(SOLO, own, LEFT, right, mp)
     pass_on(SOLO, own, RIGHT, left, mp)
-    pass_on(0, own, LEFT, right, mp)
-    pass_on(0, own, RIGHT, left, mp)
 
     for load in loads[4:7]:
         load.wait()
@@ -346,11 +346,11 @@
     own_sum[...] = near_sum(0)
 
     relay(SOLO, beside + x, BESIDE, (LEFT2, SOLO, right, mp), (RIGHT2, SOLO, left, mp))
+    relay(0, mine + left_x, LEFT, (FAR, 0, right, mp, (0, 1)))
+    relay(0, mine + right_x, RIGHT, (FAR, 0, left, mp, (2,)))
     relay(SOLO, mine + left_x, LEFT, (FAR, SOLO, right, mp))
     relay(SOLO, mine + right_x, RIGHT)
     pass_on(0, own, BESIDE, other_dp, other_mp)
-    relay(0, mine + left_x, LEFT, (FAR, 0, right, mp, (0, 1)))
-    relay(0, mine + right_x, RIGHT, (FAR, 0, left, mp, (2,)))
 
     relay(SOLO, beside + right_x, RIGHT2, (FAR2, SOLO, left, mp))
     relay(SOLO, beside + left_x, LEFT2)

time: 77 us -> 76.8 us (level)
  no operation moved by 1% of the time
where the time goes in v5:
time: 76.8 us; the launch traced here: 76.6 us
  Pallas kernels  72.7 us (95%)
  between operations  2.45 us (3%)
  local copies, waits for them, and re-layouts  1.47 us (2%)
    pallas_call x1, Pallas kernels, body(): pl.pallas_call(kernel, out_shape=(pltpu.VMEM((1, 128), F32), pltpu.VMEM((...  72.7 us

profile of v5, /device:TPU:1, one launch (start us, length us, event | category | flops | bytes accessed | tf_op | source)
XLA Modules:
  0.0 76.6 jit_solution(7196407474591843267)
XLA Ops:
  1.3 72.7 %guided_step.1 = (f32[1,128]{1,0:T(1,128)S(1)}, f32[64,160]{1,0:T(8,128)S(1)}, bf16[160,2048]{1,0:T(8,128)(2,1)S(1)}) custom-call(s32[1]{0:T(128)S(6)} %copy.16.step_ref, bf16[160,2048]{1,0:T(8,128)(2,1)} %bitcast.11, bf16[50,2,160]{2,1,0:T(2,128)(2,1)} %mod_far.1, bf16[64,160]{1,0:T(8,128)(2,1)} %bitcast.14, bf16[27,24,384]{2,1,0:T(8,128)(2,1)} %bitcast.12, ...), custom_call_target="tpu_custom_call" | custom-call | tf_op jit(solution)/shard_map/guided_step/pallas_call | solution.py:560
  74.0 0.6 copy.14
  74.6 0.8 %copy.15 = bf16[2048,160]{0,1:T(8,128)(2,1)} copy(bf16[2048,160]{0,1:T(8,128)(2,1)S(1)} %bitcast.8) | data formatting | bytes 1310720
